TPU v7x, 32 devices: a whole 2x2x4 slice. The times are simulated.
32 devices in a mesh: section: 2 (over x), dp: 4 (over y, core), tensor: 4 (over z).
Axes of the slice: x: 2, y: 2, z: 4, core: 2. Of those that a mesh axis runs over, the one named last changes fastest.
Arguments:
- hidden: bfloat16 [2, 640, 8192], P('section', 'dp', 'tensor'), may hold values from -6 to 6
- w_query: bfloat16 [2, 8192, 4096], P('section', 'dp', 'tensor'), may hold values from -0.0625 to 0.0625
- key_weight_stack: bfloat16 [2, 8192, 1024], P('section', 'tensor', 'dp'), may hold values from -0.0625 to 0.0625
- value_weight_stack: bfloat16 [2, 8192, 1024], P('section', 'tensor', 'dp'), may hold values from -0.0625 to 0.0625
- image_tokens: bfloat16 [4, 128, 8192], P('dp', 'section', 'tensor'), may hold values from -6 to 6
- score_bias: float32 [640, 128], P('dp'), may hold values from -4 to 404, as said below
- gate_logit: float32 [2], P('section'), may hold values from 0.3 to 1.5
- cotangent: bfloat16 [2, 640, 4096], P('section', 'dp', 'tensor'), may hold values from -48 to 48
Outputs:
- gated_output: bfloat16 [2, 640, 4096], P('section', 'dp', 'tensor')
- image_grad: float32 [4, 128, 8192], P('dp', 'section', 'tensor')
Inputs may be any that keep to these rules, and one draw needn't show every extreme that they name: `score_bias`: additive bias on the attention scores of each text token and image token.
All inputs are finite; a program needn't handle non-finite values.
Results may differ from a plain program's by a relative error of at most 0.0079.
Values may be sent and summed in bfloat16 or wider, within the bound.
A program may use at most 64 MiB of HBM per device.

v0:
```python
import jax
import jax.numpy as jnp
from jax import lax
from jax.sharding import PartitionSpec as P

QUERY_HEADS = 32
KEY_VALUE_HEADS = 8
HEAD_SIZE = 128


def local(
    hidden,
    w_query,
    key_weight_stack,
    value_weight_stack,
    image_tokens,
    score_bias,
    gate_logit,
    cotangent,
):
    tok_rows = hidden.shape[1]
    columns = w_query.shape[2]
    query_group_size = QUERY_HEADS // KEY_VALUE_HEADS
    local_heads = columns // HEAD_SIZE // query_group_size
    scaling = HEAD_SIZE ** (-0.5)
    features = lax.all_gather(hidden[0], "tensor", axis=1, tiled=True)
    query_input = jnp.dot(
        features,
        lax.all_gather(w_query[0], "dp", axis=0, tiled=True),
        preferred_element_type=jnp.float32,
    )
    query_input = query_input.astype(jnp.bfloat16).reshape(
        tok_rows, local_heads, query_group_size, HEAD_SIZE
    )
    image_rows = lax.all_gather(image_tokens[0], "section", axis=0, tiled=True)
    image_count = image_rows.shape[0]
    key_cols, value_cols = (
        lax.all_gather(key_weight_stack[0], "dp", axis=1, tiled=True),
        lax.all_gather(value_weight_stack[0], "dp", axis=1, tiled=True),
    )
    key_portion = jnp.dot(image_rows, key_cols, preferred_element_type=jnp.float32).reshape(
        image_count, KEY_VALUE_HEADS, 1, HEAD_SIZE
    )
    value_portion = jnp.dot(image_rows, value_cols, preferred_element_type=jnp.float32).reshape(
        image_count, KEY_VALUE_HEADS, 1, HEAD_SIZE
    )
    joined_rows = jnp.concatenate([key_portion, value_portion], axis=2).reshape(
        image_count, KEY_VALUE_HEADS * 2 * HEAD_SIZE
    )
    own_pairs = lax.psum_scatter(joined_rows, "tensor", scatter_dimension=1, tiled=True)
    own_pairs = own_pairs.astype(jnp.bfloat16).reshape(image_count, local_heads, 2, HEAD_SIZE)
    keys = own_pairs[:, :, 0]
    values = own_pairs[:, :, 1]
    scores = (
        jnp.einsum("tkgh,ikh->kgti", query_input, keys, preferred_element_type=jnp.float32)
        * scaling
    )
    scores = scores + score_bias[None, None]
    row_max = jnp.max(scores, axis=-1, keepdims=True)
    exponent = jnp.exp(scores - row_max)
    attn_weights = exponent / jnp.sum(exponent, axis=-1, keepdims=True)
    weights_low = attn_weights.astype(jnp.bfloat16)
    attended = jnp.einsum("kgti,ikh->tkgh", weights_low, values, preferred_element_type=jnp.float32)
    scale_factor = jnp.tanh(gate_logit[0])
    gated_out = (scale_factor * attended).astype(jnp.bfloat16).reshape(1, tok_rows, columns)
    attended_gradient = (scale_factor * cotangent[0].astype(jnp.float32)).astype(jnp.bfloat16)
    attended_gradient = attended_gradient.reshape(
        tok_rows, local_heads, query_group_size, HEAD_SIZE
    )
    value_gradient = jnp.einsum(
        "kgti,tkgh->ikh", weights_low, attended_gradient, preferred_element_type=jnp.float32
    ).astype(jnp.bfloat16)
    grad_weights = jnp.einsum(
        "tkgh,ikh->kgti", attended_gradient, values, preferred_element_type=jnp.float32
    )
    grad_scores = attn_weights * (
        grad_weights - jnp.sum(attn_weights * grad_weights, axis=-1, keepdims=True)
    )
    grad_low = grad_scores.astype(jnp.bfloat16)
    key_gradient = (
        jnp.einsum("kgti,tkgh->ikh", grad_low, query_input, preferred_element_type=jnp.float32)
        * scaling
    )
    key_gradient = key_gradient.astype(jnp.bfloat16)
    packed_rows = jnp.stack([key_gradient, value_gradient], axis=2).reshape(
        image_count, local_heads * 2 * HEAD_SIZE
    )
    every_gradient = lax.all_gather(packed_rows, "tensor", axis=1, tiled=True).reshape(
        image_count, KEY_VALUE_HEADS, 2, HEAD_SIZE
    )
    key_gradients = every_gradient[:, :, 0].reshape(image_count, KEY_VALUE_HEADS * HEAD_SIZE)
    value_gradients = every_gradient[:, :, 1].reshape(image_count, KEY_VALUE_HEADS * HEAD_SIZE)
    contract = (((1,), (1,)), ((), ()))
    partial_grad = lax.dot_general(
        key_gradients, key_cols, contract, preferred_element_type=jnp.float32
    )
    partial_grad = partial_grad + lax.dot_general(
        value_gradients, value_cols, contract, preferred_element_type=jnp.float32
    )
    image_grad = lax.psum_scatter(partial_grad, "section", scatter_dimension=0, tiled=True)
    return (gated_out, image_grad[None])


def solution(mesh):
    in_specs = (
        P("section", "dp", "tensor"),
        P("section", "dp", "tensor"),
        P("section", "tensor", "dp"),
        P("section", "tensor", "dp"),
        P("dp", "section", "tensor"),
        P("dp", None),
        P("section"),
        P("section", "dp", "tensor"),
    )
    out_specs = (P("section", "dp", "tensor"), P("dp", "section", "tensor"))
    return jax.shard_map(local, mesh=mesh, in_specs=in_specs, out_specs=out_specs, check_vma=False)
```

profile of v0, /device:TPU:17, one launch (start us, length us, event | category | flops | bytes accessed | tf_op | source)
XLA Modules:
  0.0 342.5 jit_solution(15440682938699365437)
XLA Ops:
  7.2 0.0 all-gather.12.cloned.1.call-start
  7.2 0.7 all-gather.12.cloned.1.call-update
  7.9 0.0 all-gather.10.cloned.1.call-start
  7.9 0.7 all-gather.10.cloned.1.call-update
  8.6 0.0 reduce-scatter.3.cloned.1.call-start
  8.7 8.1 %all-gather = bf16[1,128,2048]{2,1,0:T(8,128)(2,1)S(1)} all-gather(bf16[1,64,2048]{2,1,0:T(8,128)(2,1)} %param.12), channel_id=2, replica_groups=mesh['section'=2,'dp'=4,'tensor'=4] {'section'}, dimensions={1}, use_global_device_ids=true | all-gather | bytes 786432 | tf_op jit(solution)/shard_map/all_gather | solution.py:35
  16.8 29.3 %all-gather.12.cloned.1.call-done = bf16[1,2048,1024]{2,1,0:T(8,128)(2,1)} async-done(((bf16[1,2048,256]{2,1,0:T(8,128)(2,1)}), bf16[1,2048,1024]{2,1,0:T(8,128)(2,1)}) %all-gather.12.cloned.1.call-update) | async-done | bytes 4194320 | tf_op jit(solution)/shard_map/all_gather | solution.py:39
  46.1 3.9 %fusion.5 = f32[128,1024]{0,1:T(8,128)S(1)} fusion(bf16[1,2048,1024]{2,1,0:T(8,128)(2,1)} %all-gather.12.cloned.1.call-done, bf16[1,128,2048]{2,1,0:T(8,128)(2,1)S(1)} %all-gather), kind=kOutput, calls=%fused_computation.5 | convolution fusion | flops 536870912 | bytes 5242880 | tf_op jit(solution)/shard_map/reshape | solution.py:44
  50.0 32.7 %all-gather.10.cloned.1.call-done = bf16[1,2048,1024]{2,1,0:T(8,128)(2,1)} async-done(((bf16[1,2048,256]{2,1,0:T(8,128)(2,1)}), bf16[1,2048,1024]{2,1,0:T(8,128)(2,1)}) %all-gather.10.cloned.1.call-update) | async-done | bytes 4194320 | tf_op jit(solution)/shard_map/all_gather | solution.py:38
  82.7 3.9 %fusion.9 = f32[128,1024]{0,1:T(8,128)S(1)} fusion(bf16[1,2048,1024]{2,1,0:T(8,128)(2,1)} %all-gather.10.cloned.1.call-done, bf16[1,128,2048]{2,1,0:T(8,128)(2,1)S(1)} %all-gather), kind=kOutput, calls=%fused_computation.9 | convolution fusion | flops 536870912 | bytes 5242880 | tf_op jit(solution)/shard_map/reshape | solution.py:41
  86.6 0.0 copy-start.1
  86.7 1.1 pad_maximum_fusion
  87.7 0.0 reduce-scatter.3.cloned.1.call-update
  87.8 0.0 all-gather.14.cloned.1.call-start
  87.8 0.5 all-gather.14.cloned.1.call-update
  88.4 0.0 all-gather.16.cloned.1.call-start
  88.4 0.5 all-gather.16.cloned.1.call-update
  88.9 0.0 reduce-scatter.5.cloned.1.call-start
  89.7 0.0 copy-done.1
  89.7 0.1 multiply_convert_fusion.1
  89.7 0.2 convert_element_type.49
  90.0 23.4 %reduce-scatter.3.cloned.1.call-done = f32[128,512]{0,1:T(8,128)} async-done(((f32[128,2048]{0,1:T(8,128)}), f32[128,512]{0,1:T(8,128)}) %reduce-scatter.3.cloned.1.call-update) | async-done | bytes 262160 | tf_op jit(solution)/shard_map/reduce_scatter | solution.py:50
  113.3 1.0 convert_element_type.42
  114.3 0.0 copy-start.2
  114.3 54.1 %all-gather.14.cloned.1.call-done = bf16[1,160,8192]{2,1,0:T(8,128)(2,1)} async-done(((bf16[1,160,2048]{2,1,0:T(8,128)(2,1)}), bf16[1,160,8192]{2,1,0:T(8,128)(2,1)}) %all-gather.14.cloned.1.call-update) | async-done | bytes 2621456 | tf_op jit(solution)/shard_map/all_gather | solution.py:26
  168.4 107.9 %all-gather.16.cloned.1.call-done = bf16[1,8192,1024]{2,1,0:T(8,128)(2,1)} async-done(((bf16[1,2048,1024]{2,1,0:T(8,128)(2,1)}), bf16[1,8192,1024]{2,1,0:T(8,128)(2,1)}) %all-gather.16.cloned.1.call-update) | async-done | bytes 16777232 | tf_op jit(solution)/shard_map/all_gather | solution.py:29
  276.3 9.4 %fusion.20 = bf16[160,1024]{1,0:T(8,128)(2,1)S(1)} fusion(bf16[1,8192,1024]{2,1,0:T(8,128)(2,1)} %all-gather.16.cloned.1.call-done, bf16[1,160,8192]{2,1,0:T(8,128)(2,1)} %all-gather.14.cloned.1.call-done), kind=kOutput, calls=%fused_computation.21 | convolution fusion | flops 2684518400 | bytes 19726336 | tf_op jit(solution)/shard_map/dot_general | solution.py:27
  285.7 0.2 reshape.43
  285.9 0.0 copy-done.2
  286.0 0.7 fusion.59
  286.7 2.5 fusion.29
  289.2 0.6 multiply_reduce_fusion
  289.8 2.7 fusion.30
  292.5 0.0 copy-start
  292.5 13.4 %all_gather.23 = bf16[128,2048]{0,1:T(8,128)(2,1)S(1)} all-gather(bf16[128,512]{0,1:T(8,128)(2,1)S(1)} %bitcast.135), channel_id=1, replica_groups=mesh['section'=2,'dp'=4,'tensor'=4] {'tensor'}, dimensions={1}, use_global_device_ids=true | all-gather | bytes 655360 | tf_op jit(solution)/shard_map/all_gather | solution.py:88
  306.0 3.7 %fusion.3 = f32[128,2048]{1,0:T(8,128)S(1)} fusion(bf16[128,1024]{0,1:T(8,128)(2,1)S(1)} %bitcast.134, bf16[1,2048,1024]{2,1,0:T(8,128)(2,1)} %all-gather.12.cloned.1.call-done), kind=kOutput, calls=%fused_computation.3 | convolution fusion | flops 536870912 | bytes 5505024 | tf_op jit(solution)/shard_map/dot_general | solution.py:97
  309.7 0.0 copy-done
  309.7 2.5 fusion.12
  312.2 0.0 reduce-scatter.5.cloned.1.call-update
  312.3 2.3 fusion.25
  314.5 0.2 copy.19
  314.7 0.9 reshape.44
  315.7 20.0 %reduce-scatter.5.cloned.1.call-done = f32[64,2048]{1,0:T(8,128)} async-done(((f32[128,2048]{1,0:T(8,128)}), f32[64,2048]{1,0:T(8,128)}) %reduce-scatter.5.cloned.1.call-update) | async-done | bytes 524304 | tf_op jit(solution)/shard_map/reduce_scatter | solution.py:100
  (3 shorter events, 0.1 us)
Async XLA Ops:
  7.2 38.9 %all-gather.12.cloned.1.call-start = ((), (), s32[]{:S(2)}) async-start(), calls=%async_computation.5 | async-start | bytes 5242880 | tf_op jit(solution)/shard_map/all_gather | solution.py:39
  7.9 74.8 %all-gather.10.cloned.1.call-start = ((), (), s32[]{:S(2)}) async-start(), calls=%async_computation.4 | async-start | bytes 5242880 | tf_op jit(solution)/shard_map/all_gather | solution.py:38
  8.6 104.7 %reduce-scatter.3.cloned.1.call-start = ((), (), s32[]{:S(2)}) async-start(), calls=%async_computation.2 | async-start | bytes 1310720 | tf_op jit(solution)/shard_map/reduce_scatter | solution.py:50
  86.6 3.0 copy-start.1
  87.8 80.6 %all-gather.14.cloned.1.call-start = ((), (), s32[]{:S(2)}) async-start(), calls=%async_computation.6 | async-start | bytes 3276800 | tf_op jit(solution)/shard_map/all_gather | solution.py:26
  88.4 187.9 %all-gather.16.cloned.1.call-start = ((), (), s32[]{:S(2)}) async-start(), calls=%async_computation.7 | async-start | bytes 20971520 | tf_op jit(solution)/shard_map/all_gather | solution.py:29
  88.9 246.7 %reduce-scatter.5.cloned.1.call-start = ((), (), s32[]{:S(2)}) async-start(), calls=%async_computation.3 | async-start | bytes 1572864 | tf_op jit(solution)/shard_map/reduce_scatter | solution.py:100
  114.3 171.6 %copy-start.2 = (f32[160,128]{1,0:T(8,128)S(1)}, f32[160,128]{1,0:T(8,128)}, u32[]{:S(2)}) copy-start(f32[160,128]{1,0:T(8,128)} %param.13) | copy-start | bytes 245764
  292.5 17.3 %copy-start = (bf16[1,2048,1024]{2,1,0:T(8,128)(2,1)S(1)}, bf16[1,2048,1024]{2,1,0:T(8,128)(2,1)}, u32[]{:S(2)}) copy-start(bf16[1,2048,1024]{2,1,0:T(8,128)(2,1)} %all-gather.10.cloned.1.call-done) | copy-start | bytes 12582916
Sparse Core Ops, SparseCore 0:
  9.5 36.5 all-gather.11
  47.7 35.0 all-gather.9
  87.9 25.3 reduce-scatter.2
  114.8 53.5 all-gather.13
  169.9 106.3 all-gather.15
  312.4 23.2 reduce-scatter.4
where the time goes:
time: 344 us; the launch traced here: 342 us
  waiting for transfers between devices  270 us (78%)
  matrix products  32.3 us (9%)
  blocking collectives  21.5 us (6%)
  between operations  14.9 us (4%)
    all_gather x1, waiting for transfers between devices, local(): lax.all_gather(w_query[0], 'dp', axis=0, tiled=True)  108 us
    all_gather x1, waiting for transfers between devices, local(): features = lax.all_gather(hidden[0], 'tensor', axis=1, tiled=True)  54.1 us
    all_gather x1, waiting for transfers between devices, local(): lax.all_gather(key_weight_stack[0], 'dp', axis=1, tiled=True)  32.7 us
    all_gather x1, waiting for transfers between devices, local(): lax.all_gather(value_weight_stack[0], 'dp', axis=1, tiled=True)  29.3 us
    reduce_scatter x1, waiting for transfers between devices, local(): lax.psum_scatter(joined_rows, 'tensor', scatter_dimension=1, tiled=True)  23.4 us
    reduce_scatter x1, waiting for transfers between devices, local(): lax.psum_scatter(partial_grad, 'section', scatter_dimension=0, tiled=True)  20 us
    all_gather x1, blocking collectives, local(): lax.all_gather(packed_rows, 'tensor', axis=1, tiled=True)  13.4 us
    dot_general x1, matrix products, local(): jnp.dot(features, lax.all_gather(w_query[0], 'dp', axis=0, tiled=True), p...  9.44 us
  transfers between devices with their start and end apart: 6, of which 6 were waited for; matrix products, arithmetic and copies ran while one was open for 3% of the time, Pallas kernels for 0%

commit v1 on v0

v1 whole, which is shorter than its diff:
```python
import functools

import jax
import jax.numpy as jnp
from jax import lax
from jax.experimental import pallas as pl
from jax.experimental.pallas import tpu as pltpu
from jax.sharding import PartitionSpec as P

HEAD_SIZE = 128
QUERY_GROUP = 4
CORES = 2
BF16 = jnp.bfloat16
F32 = jnp.float32
NT = (((1,), (1,)), ((), ()))
TN = (((0,), (0,)), ((), ()))


def remote(src, dst, send_sem, recv_sem, device):
    return pltpu.make_async_remote_copy(
        src_ref=src,
        dst_ref=dst,
        send_sem=send_sem,
        recv_sem=recv_sem,
        device_id=device,
        device_id_type=pl.DeviceIdType.MESH,
    )


def kernel(
    sizes, hidden, w_query, key_w, value_w, image, bias, gate, cotangent, out, grad,
    wq, wkv, img, cot, hb, pb, kvr, kvs, qsib, qsr, qsend, qr, qacc, qs, gb, fsib, fsr, fsend, fr,
    load, ix_s, ix_r, iy_s, iy_r, ic_s, ic_r, hr_s, hl_s, h_r, hx_s, hx_r, p_s, p_r, kv_s, kv_r,
    qc_s, qc_r, qy_s, qy_r, g_s, g_r, gx_s, gx_r, fc_s, fc_r, f_s, f_r,
):
    S, D, T = sizes
    Y = D // CORES
    s, d, t = lax.axis_index("section"), lax.axis_index("dp"), lax.axis_index("tensor")
    y, c = d // CORES, d % CORES
    sibling = y * CORES + 1 - c
    rows = image.shape[0]
    image_count = S * rows
    kc = key_w.shape[1]
    width = wq.shape[1]
    feats = wq.shape[0]
    qtile = min(256, width)
    waits = []

    def load_copy(i, src, dst):
        copy = pltpu.make_async_copy(src, dst, load.at[i])
        copy.start()
        return copy

    own_rows = pl.ds(pl.multiple_of(d * image_count + s * rows, rows), rows)
    load_image = load_copy(0, image, img.at[own_rows])
    load_hidden = load_copy(1, hidden, hb.at[t])
    load_key = load_copy(2, key_w, wkv.at[:, pl.ds(0, kc)])
    load_value = load_copy(3, value_w, wkv.at[:, pl.ds(kc, kc)])
    load_query = load_copy(4, w_query, wq)
    load_cot = load_copy(5, cotangent, cot)

    others = [{"dp": lax.rem(d + j, D)} for j in range(1, D)]
    others += [{"tensor": lax.rem(t + j, T)} for j in range(1, T)]
    for i in range(1, S):
        for j in range(Y):
            others.append(
                {"section": lax.rem(s + i, S), "dp": lax.rem(y + j, Y) * CORES + c}
            )
    barrier = pltpu.get_barrier_semaphore()
    for device in others:
        pl.semaphore_signal(
            barrier, inc=1, device_id=device, device_id_type=pl.DeviceIdType.MESH
        )
    pl.semaphore_wait(barrier, len(others))

    load_image.wait()
    for i in range(1, S):
        to = lax.rem(s + i, S)
        copy = remote(
            img.at[own_rows], img.at[own_rows], ix_s.at[to], ix_r.at[s], {"section": to}
        )
        copy.start()
        waits.append(copy.wait_send)

    load_hidden.wait()

    def right(f):
        return remote(hb.at[f], hb.at[f], hr_s.at[f], h_r.at[f], {"tensor": t + 1})

    def left(f):
        return remote(hb.at[f], hb.at[f], hl_s.at[f], h_r.at[f], {"tensor": t - 1})

    def across(f):
        return remote(hb.at[f], hb.at[T + d], hx_s.at[f], hx_r.at[d], {"dp": f})

    def hidden_arrive(k):
        if k == 0:
            return
        pl.when(t - k >= 0)(lambda: right(t - k).wait_recv())
        pl.when(t + k < T)(lambda: left(t + k).wait_recv())

    def hidden_pass(k):
        if k < T - 1:
            pl.when((t - k >= 0) & (t + 1 < T))(lambda: right(t - k).start())
            pl.when((t + k < T) & (t >= 1))(lambda: left(t + k).start())
        if k == 0:
            pl.when(t != d)(lambda: across(t).start())
        else:
            pl.when((t - k >= 0) & (t - k != d))(lambda: across(t - k).start())
            pl.when((t + k < T) & (t + k != d))(lambda: across(t + k).start())

    hidden_pass(0)

    def image_block(n):
        return img.at[pl.ds(pl.multiple_of(n * image_count, image_count), image_count)]

    for i in range(1, S):
        src = lax.rem(s + i, S)
        block = img.at[pl.ds(pl.multiple_of(d * image_count + src * rows, rows), rows)]
        remote(block, block, ix_s.at[src], ix_r.at[src], {"section": src}).wait_recv()
    for j in range(1, Y):
        to = lax.rem(y + j, Y)
        copy = remote(
            image_block(d), image_block(d), iy_s.at[to], iy_r.at[y], {"dp": to * CORES + c}
        )
        copy.start()
        waits.append(copy.wait_send)

    def to_sibling(n, slot):
        copy = remote(image_block(n), image_block(n), ic_s.at[slot], ic_r.at[slot], {"dp": sibling})
        copy.start()
        waits.append(copy.wait_send)

    to_sibling(d, y)
    for j in range(1, Y):
        src = lax.rem(y + j, Y)
        n = src * CORES + c
        remote(
            image_block(n), image_block(n), iy_s.at[src], iy_r.at[src], {"dp": n}
        ).wait_recv()
        to_sibling(n, src)

    hidden_arrive(1)
    hidden_pass(1)

    for j in range(Y):
        n = j * CORES + 1 - c
        remote(
            image_block(n), image_block(n), ic_s.at[j], ic_r.at[j], {"dp": sibling}
        ).wait_recv()
    load_key.wait()
    load_value.wait()
    ptile = min(256, 2 * kc)

    @pl.loop(0, 2 * kc // ptile)
    def _(i):
        columns = pl.ds(pl.multiple_of(i * ptile, ptile), ptile)
        part = jnp.dot(img[...], wkv[:, columns], preferred_element_type=F32).astype(BF16)
        for n in range(D):
            pb[n, :, columns] = part[n * image_count : (n + 1) * image_count]

    for j in range(1, D):
        n = lax.rem(d + j, D)
        copy = remote(pb.at[n], pb.at[D + d], p_s.at[n], p_r.at[d], {"dp": n})
        copy.start()
        waits.append(copy.wait_send)

    for k in range(2, T - 1):
        hidden_arrive(k)
        hidden_pass(k)

    for j in range(1, D):
        n = lax.rem(d + j, D)
        remote(pb.at[n], pb.at[D + n], p_s.at[n], p_r.at[n], {"dp": n}).wait_recv()
    for j in range(1, T):
        f = lax.rem(t + j, T)
        copy = remote(
            pb.at[jnp.where(f == d, f, D + f)], kvr.at[t], kv_s.at[f], kv_r.at[t], {"tensor": f}
        )
        copy.start()
        waits.append(copy.wait_send)

    hidden_arrive(T - 1)
    hidden_pass(T - 1)

    load_query.wait()

    def tokens_of(n):
        if n is None:
            return hb.at[d]
        remote(hb.at[0], hb.at[T + n], hx_s.at[0], hx_r.at[n], {"dp": n}).wait_recv()
        return hb.at[T + n]

    order = list(range(1, Y)) + [0]
    for j in order:
        yy = lax.rem(y + j, Y)
        block = tokens_of(yy * CORES + 1 - c)

        @pl.loop(0, width // qtile)
        def _(i):
            columns = pl.ds(pl.multiple_of(i * qtile, qtile), qtile)
            qsib[yy, :, columns] = jnp.dot(
                block[...], wq[:, columns], preferred_element_type=F32
            ).astype(BF16)

        copy = remote(qsib.at[yy], qsr.at[yy], qc_s.at[yy], qc_r.at[yy], {"dp": sibling})
        copy.start()
        waits.append(copy.wait_send)
    for j in order:
        yy = lax.rem(y + j, Y)
        block = tokens_of(None if j == 0 else yy * CORES + c)
        remote(qsib.at[yy], qsr.at[yy], qc_s.at[yy], qc_r.at[yy], {"dp": sibling}).wait_recv()

        @pl.loop(0, width // qtile)
        def _(i):
            columns = pl.ds(pl.multiple_of(i * qtile, qtile), qtile)
            part = jnp.dot(block[...], wq[:, columns], preferred_element_type=F32)
            part = part + qsr[yy, :, columns].astype(F32)
            if j:
                qsend[yy, :, columns] = part.astype(BF16)
            else:
                qacc[:, columns] = part

        if j:
            copy = remote(
                qsend.at[yy], qr.at[y], qy_s.at[yy], qy_r.at[y], {"dp": yy * CORES + c}
            )
            copy.start()
            waits.append(copy.wait_send)

    total = pb[jnp.where(t == d, t, D + t)].astype(F32)
    for j in range(1, T):
        f = lax.rem(t + j, T)
        remote(kvr.at[f], kvr.at[f], kv_s.at[f], kv_r.at[f], {"tensor": f}).wait_recv()
        total = total + kvr[f].astype(F32)
    kvs[...] = total.astype(BF16)
    load_cot.wait()

    query = qacc[...]
    for j in range(1, Y):
        yy = lax.rem(y + j, Y)
        remote(
            qsend.at[yy], qr.at[yy], qy_s.at[yy], qy_r.at[yy], {"dp": yy * CORES + c}
        ).wait_recv()
        query = query + qr[yy].astype(F32)
    qs[...] = query.astype(BF16)

    scaling = HEAD_SIZE ** (-0.5)
    tokens = bias.shape[0]
    scale = jnp.tanh(jnp.full((1, HEAD_SIZE), gate[0], F32))
    bias_rows = jnp.concatenate([bias[...]] * QUERY_GROUP, axis=0)
    for k in range(kc // HEAD_SIZE):
        key = kvs[:, k * HEAD_SIZE : (k + 1) * HEAD_SIZE]
        value = kvs[:, kc + k * HEAD_SIZE : kc + (k + 1) * HEAD_SIZE]
        heads = [
            slice((k * QUERY_GROUP + g) * HEAD_SIZE, (k * QUERY_GROUP + g + 1) * HEAD_SIZE)
            for g in range(QUERY_GROUP)
        ]
        stacked = jnp.concatenate([qs[:, h] for h in heads], axis=0)
        above = jnp.concatenate([cot[:, h] for h in heads], axis=0)
        above = (scale * above.astype(F32)).astype(BF16)
        scores = lax.dot_general(stacked, key, NT, preferred_element_type=F32) * scaling
        scores = scores + bias_rows
        exponent = jnp.exp(scores - jnp.max(scores, axis=-1, keepdims=True))
        weights = exponent / jnp.sum(exponent, axis=-1, keepdims=True)
        low = weights.astype(BF16)
        attended = scale * jnp.dot(low, value, preferred_element_type=F32)
        for g, h in enumerate(heads):
            out[:, h] = attended[g * tokens : (g + 1) * tokens].astype(BF16)
        value_grad = lax.dot_general(low, above, TN, preferred_element_type=F32)
        grad_weights = lax.dot_general(above, value, NT, preferred_element_type=F32)
        mean = jnp.sum(weights * grad_weights, axis=-1, keepdims=True)
        grad_low = (weights * (grad_weights - mean)).astype(BF16)
        key_grad = lax.dot_general(grad_low, stacked, TN, preferred_element_type=F32) * scaling
        gb[t, :, k * HEAD_SIZE : (k + 1) * HEAD_SIZE] = key_grad.astype(BF16)
        gb[t, :, kc + k * HEAD_SIZE : kc + (k + 1) * HEAD_SIZE] = value_grad.astype(BF16)

    for j in range(1, T):
        f = lax.rem(t + j, T)
        copy = remote(gb.at[t], gb.at[t], g_s.at[f], g_r.at[t], {"tensor": f})
        copy.start()
        waits.append(copy.wait_send)

    def grad_across(f):
        return remote(gb.at[f], gb.at[T + d], gx_s.at[f], gx_r.at[d], {"dp": f})

    def grad_arrive(f):
        remote(gb.at[f], gb.at[f], g_s.at[f], g_r.at[f], {"tensor": f}).wait_recv()
        pl.when(f != d)(lambda: grad_across(f).start())

    pl.when(t != d)(lambda: grad_across(t).start())
    for k in range(1, T):
        pl.when(t - k >= 0)(functools.partial(grad_arrive, t - k))
        pl.when(t + k < T)(functools.partial(grad_arrive, t + k))

    def grads_of(n):
        if n is None:
            return gb[d]
        remote(gb.at[0], gb.at[T + n], gx_s.at[0], gx_r.at[n], {"dp": n}).wait_recv()
        return gb[T + n]

    ftile = min(512, feats)
    for j in order:
        yy = lax.rem(y + j, Y)
        block = grads_of(yy * CORES + 1 - c)

        @pl.loop(0, feats // ftile)
        def _(i):
            columns = pl.ds(pl.multiple_of(i * ftile, ftile), ftile)
            fsib[yy, :, columns] = lax.dot_general(
                block, wkv[columns, :], NT, preferred_element_type=F32
            ).astype(BF16)

        copy = remote(fsib.at[yy], fsr.at[yy], fc_s.at[yy], fc_r.at[yy], {"dp": sibling})
        copy.start()
        waits.append(copy.wait_send)
    sections = list(range(1, S)) + [0]
    for j in order:
        yy = lax.rem(y + j, Y)
        block = grads_of(None if j == 0 else yy * CORES + c)
        remote(fsib.at[yy], fsr.at[yy], fc_s.at[yy], fc_r.at[yy], {"dp": sibling}).wait_recv()

        @pl.loop(0, feats // ftile)
        def _(i):
            columns = pl.ds(pl.multiple_of(i * ftile, ftile), ftile)
            part = lax.dot_general(block, wkv[columns, :], NT, preferred_element_type=F32)
            part = part + fsr[yy, :, columns].astype(F32)
            fsend[yy, :, columns] = part

        for i in sections:
            if i == 0 and j == 0:
                continue
            ss = lax.rem(s + i, S)
            span = pl.ds(pl.multiple_of(ss * rows, rows), rows)
            fsib_out = fr.at[0, yy, ss]
            fsib_out[...] = fsend[yy, span, :].astype(BF16)
            copy = remote(
                fsib_out, fr.at[1, y, s], f_s.at[yy, ss], f_r.at[y, s],
                {"section": ss, "dp": yy * CORES + c},
            )
            copy.start()
            waits.append(copy.wait_send)
    result = fsend[y, pl.ds(pl.multiple_of(s * rows, rows), rows), :]
    for j in order:
        yy = lax.rem(y + j, Y)
        for i in sections:
            if i == 0 and j == 0:
                continue
            ss = lax.rem(s + i, S)
            slot = fr.at[1, yy, ss]
            remote(
                slot, slot, f_s.at[yy, ss], f_r.at[yy, ss],
                {"section": ss, "dp": yy * CORES + c},
            ).wait_recv()
            result = result + slot[...].astype(F32)
    grad[...] = result

    for wait in waits:
        wait()
    for k in range(T):
        if k < T - 1:
            pl.when((t - k >= 0) & (t + 1 < T))(lambda: right(t - k).wait_send())
            pl.when((t + k < T) & (t >= 1))(lambda: left(t + k).wait_send())
    for f in range(T):
        pl.when(f != d)(lambda: across(f).wait_send())
        pl.when(f != d)(lambda: grad_across(f).wait_send())


def local(sizes, hidden, w_query, key_w, value_w, image, bias, gate, cotangent):
    S, D, T = sizes
    Y = D // CORES
    tokens, feats = hidden.shape[1:]
    width = w_query.shape[2]
    kc = key_w.shape[2]
    rows = image.shape[1]
    images = S * rows
    sem = lambda *n: pltpu.SemaphoreType.DMA(n)
    any_space = pl.BlockSpec(memory_space=pl.ANY)
    vmem = pl.BlockSpec(memory_space=pltpu.VMEM)
    smem = pl.BlockSpec(memory_space=pltpu.SMEM)
    out, grad = pl.pallas_call(
        functools.partial(kernel, sizes),
        out_shape=(
            jax.ShapeDtypeStruct((tokens, width), BF16),
            jax.ShapeDtypeStruct((rows, feats), F32),
        ),
        in_specs=[any_space] * 5 + [vmem, smem, any_space],
        out_specs=(vmem, vmem),
        scratch_shapes=[
            pltpu.VMEM((feats, width), BF16),
            pltpu.VMEM((feats, 2 * kc), BF16),
            pltpu.VMEM((D * images, feats), BF16),
            pltpu.VMEM((tokens, width), BF16),
            pltpu.VMEM((T + D, tokens, feats), BF16),
            pltpu.VMEM((2 * D, images, 2 * kc), BF16),
            pltpu.VMEM((T, images, 2 * kc), BF16),
            pltpu.VMEM((images, 2 * kc), BF16),
            pltpu.VMEM((Y, tokens, width), BF16),
            pltpu.VMEM((Y, tokens, width), BF16),
            pltpu.VMEM((Y, tokens, width), BF16),
            pltpu.VMEM((Y, tokens, width), BF16),
            pltpu.VMEM((tokens, width), F32),
            pltpu.VMEM((tokens, width), BF16),
            pltpu.VMEM((T + D, images, 2 * kc), BF16),
            pltpu.VMEM((Y, images, feats), BF16),
            pltpu.VMEM((Y, images, feats), BF16),
            pltpu.VMEM((Y, images, feats), F32),
            pltpu.VMEM((2, Y, S, rows, feats), BF16),
            sem(6),
            sem(S), sem(S), sem(Y), sem(Y), sem(Y), sem(Y),
            sem(T), sem(T), sem(T), sem(T), sem(D),
            sem(D), sem(D), sem(T), sem(T),
            sem(Y), sem(Y), sem(Y), sem(Y),
            sem(T), sem(T), sem(T), sem(D),
            sem(Y), sem(Y), sem(Y, S), sem(Y, S),
        ],
        compiler_params=pltpu.CompilerParams(
            collective_id=0, has_side_effects=True, vmem_limit_bytes=52 * 1024 * 1024
        ),
    )(hidden[0], w_query[0], key_w[0], value_w[0], image[0], bias, gate, cotangent[0])
    return out[None], grad[None]


def solution(mesh):
    sizes = tuple(mesh.shape[name] for name in ("section", "dp", "tensor"))
    assert sizes[1] == sizes[2] and sizes[1] % CORES == 0
    in_specs = (
        P("section", "dp", "tensor"),
        P("section", "dp", "tensor"),
        P("section", "tensor", "dp"),
        P("section", "tensor", "dp"),
        P("dp", "section", "tensor"),
        P("dp", None),
        P("section"),
        P("section", "dp", "tensor"),
    )
    out_specs = (P("section", "dp", "tensor"), P("dp", "section", "tensor"))
    return jax.shard_map(
        functools.partial(local, sizes),
        mesh=mesh, in_specs=in_specs, out_specs=out_specs, check_vma=False,
    )
```

time: 344 us -> 131 us (0.38)
  the two profiles are of different devices: /device:TPU:17 before, /device:TPU:25 now
where the time goes in v1:
time: 131 us
  Pallas kernels  125 us (95%)
  local copies, waits for them, and re-layouts  4.32 us (3%)
    pallas_call x1, Pallas kernels, local(): pl.pallas_call(functools.partial(kernel, sizes), out_shape=(jax.ShapeDtyp...  125 us
    unnamed x8, local copies, waits for them, and re-layouts  4.32 us

profile of v1, /device:TPU:25, one launch (start us, length us, event | category | flops | bytes accessed | tf_op | source)
XLA Modules:
  0.0 130.7 jit_solution(7183880987216422504)
XLA Ops:
  1.3 0.0 copy-start
  1.3 1.0 copy-done
  2.3 0.0 copy-start.1
  2.3 0.9 copy-done.1
  3.2 0.0 copy-start.2
  3.2 0.9 copy-done.2
  4.1 125.1 %shard_map.95 = (bf16[160,1024]{1,0:T(8,128)(2,1)S(1)}, f32[64,2048]{1,0:T(8,128)S(1)}) custom-call(bf16[160,2048]{1,0:T(8,128)(2,1)} %bitcast.15, bf16[2048,1024]{1,0:T(8,128)(2,1)} %bitcast.12, bf16[2048,256]{1,0:T(8,128)(2,1)} %bitcast.13, bf16[2048,256]{1,0:T(8,128)(2,1)} %bitcast.14, bf16[64,2048]{1,0:T(8,128)(2,1)S(1)} %bitcast.11, ...), custom_call_target="tpu_custom_call" | custom-call | tf_op jit(solution)/shard_map/pallas_call | solution.py:381
  129.2 0.7 copy.13
  130.0 0.8 copy.14
Async XLA Ops:
  1.3 1.0 copy-start
  2.3 0.9 copy-start.1
  3.2 0.9 copy-start.2

commit v2 on v1

v2 whole, which is shorter than its diff:
```python
import functools

import jax
import jax.numpy as jnp
from jax import lax
from jax.experimental import pallas as pl
from jax.experimental.pallas import tpu as pltpu
from jax.sharding import PartitionSpec as P

HEAD_SIZE = 128
QUERY_GROUP = 4
HIDDEN_PARTS = 2
GRAD_PARTS = 2
CORES = 2
BF16 = jnp.bfloat16
F32 = jnp.float32
NT = (((1,), (1,)), ((), ()))
TN = (((0,), (0,)), ((), ()))


def remote(src, dst, send_sem, recv_sem, device):
    return pltpu.make_async_remote_copy(
        src_ref=src,
        dst_ref=dst,
        send_sem=send_sem,
        recv_sem=recv_sem,
        device_id=device,
        device_id_type=pl.DeviceIdType.MESH,
    )


def kernel(
    sizes, hidden, w_query, key_w, value_w, image, bias, gate, cotangent, out, grad,
    wq, wkv, img, cot, hb, pb, kvr, kvs, qsib, qsr, qsend, qr, qacc, above, wgrad, lows, gb, fsib, fsr, fsum, fsend, fr,
    load, ix_s, ix_r, iy_s, iy_r, ic_s, ic_r, hr_s, hl_s, h_r, hx_s, hx_r, p_s, p_r, kv_s, kv_r,
    qc_s, qc_r, qy_s, qy_r, g_s, g_r, gx_s, gx_r, fc_s, fc_r, f_s, f_r,
):
    S, D, T = sizes
    Y = D // CORES
    s, d, t = lax.axis_index("section"), lax.axis_index("dp"), lax.axis_index("tensor")
    y, c = d // CORES, d % CORES
    sibling = y * CORES + 1 - c
    rows = image.shape[0]
    image_count = S * rows
    kc = key_w.shape[1]
    width = wq.shape[1]
    feats = wq.shape[0]
    heads_here = kc // HEAD_SIZE
    pair = 2 * HEAD_SIZE
    span = QUERY_GROUP * HEAD_SIZE
    tokens = bias.shape[0]
    part_rows = tokens // HIDDEN_PARTS
    part_feats = feats // GRAD_PARTS
    waits = []

    def load_copy(i, src, dst):
        copy = pltpu.make_async_copy(src, dst, load.at[i])
        copy.start()
        return copy

    own_rows = pl.ds(pl.multiple_of(d * image_count + s * rows, rows), rows)
    load_image = load_copy(0, image, img.at[own_rows])
    load_hidden = load_copy(1, hidden, hb.at[t])
    load_query = load_copy(2, w_query, wq)
    load_cot = load_copy(3, cotangent, cot)
    load_pairs = []
    for k in range(heads_here):
        head = pl.ds(k * HEAD_SIZE, HEAD_SIZE)
        load_pairs += [
            load_copy(4 + 2 * k, key_w.at[:, head], wkv.at[:, pl.ds(k * pair, HEAD_SIZE)]),
            load_copy(
                5 + 2 * k, value_w.at[:, head], wkv.at[:, pl.ds(k * pair + HEAD_SIZE, HEAD_SIZE)]
            ),
        ]

    others = [{"dp": lax.rem(d + j, D)} for j in range(1, D)]
    others += [{"tensor": lax.rem(t + j, T)} for j in range(1, T)]
    for i in range(1, S):
        for j in range(Y):
            others.append(
                {"section": lax.rem(s + i, S), "dp": lax.rem(y + j, Y) * CORES + c}
            )
    barrier = pltpu.get_barrier_semaphore()
    for device in others:
        pl.semaphore_signal(
            barrier, inc=1, device_id=device, device_id_type=pl.DeviceIdType.MESH
        )
    pl.semaphore_wait(barrier, len(others))

    load_image.wait()
    for i in range(1, S):
        to = lax.rem(s + i, S)
        copy = remote(
            img.at[own_rows], img.at[own_rows], ix_s.at[to], ix_r.at[s], {"section": to}
        )
        copy.start()
        waits.append(copy.wait_send)

    load_hidden.wait()

    def piece(f, h):
        return hb.at[f, pl.ds(h * part_rows, part_rows)]

    def right(f, h):
        return remote(piece(f, h), piece(f, h), hr_s.at[f, h], h_r.at[f, h], {"tensor": t + 1})

    def left(f, h):
        return remote(piece(f, h), piece(f, h), hl_s.at[f, h], h_r.at[f, h], {"tensor": t - 1})

    def across(f, h):
        return remote(piece(f, h), piece(T + d, h), hx_s.at[f, h], hx_r.at[d, h], {"dp": f})

    def hidden_arrive(k, h):
        pl.when(t - k >= 0)(lambda: right(t - k, h).wait_recv())
        pl.when(t + k < T)(lambda: left(t + k, h).wait_recv())

    def hidden_pass(k, h):
        if k < T - 1:
            pl.when((t - k >= 0) & (t + 1 < T))(lambda: right(t - k, h).start())
            pl.when((t + k < T) & (t >= 1))(lambda: left(t + k, h).start())
        if k:
            pl.when((t - k >= 0) & (t - k != d))(lambda: across(t - k, h).start())
            pl.when((t + k < T) & (t + k != d))(lambda: across(t + k, h).start())

    def hidden_step(k, h):
        hidden_arrive(k, h)
        hidden_pass(k, h)

    for h in range(HIDDEN_PARTS):
        hidden_pass(0, h)

    def image_block(n):
        return img.at[pl.ds(pl.multiple_of(n * image_count, image_count), image_count)]

    for i in range(1, S):
        src = lax.rem(s + i, S)
        block = img.at[pl.ds(pl.multiple_of(d * image_count + src * rows, rows), rows)]
        remote(block, block, ix_s.at[src], ix_r.at[src], {"section": src}).wait_recv()
    for j in range(1, Y):
        to = lax.rem(y + j, Y)
        copy = remote(
            image_block(d), image_block(d), iy_s.at[to], iy_r.at[y], {"dp": to * CORES + c}
        )
        copy.start()
        waits.append(copy.wait_send)

    def to_sibling(n, slot):
        copy = remote(image_block(n), image_block(n), ic_s.at[slot], ic_r.at[slot], {"dp": sibling})
        copy.start()
        waits.append(copy.wait_send)

    to_sibling(d, y)
    for h in range(HIDDEN_PARTS):
        pl.when(t != d)(lambda: across(t, h).start())
    for h in range(HIDDEN_PARTS):
        hidden_step(1, h)
    for j in range(1, Y):
        src = lax.rem(y + j, Y)
        n = src * CORES + c
        remote(
            image_block(n), image_block(n), iy_s.at[src], iy_r.at[src], {"dp": n}
        ).wait_recv()
        to_sibling(n, src)

    for k in range(2, T - 1):
        hidden_step(k, 0)
    for j in range(Y):
        n = j * CORES + 1 - c
        remote(
            image_block(n), image_block(n), ic_s.at[j], ic_r.at[j], {"dp": sibling}
        ).wait_recv()
    for load_pair in load_pairs:
        load_pair.wait()
    ptile = min(256, 2 * kc)

    @pl.loop(0, 2 * kc // ptile)
    def _(i):
        columns = pl.ds(pl.multiple_of(i * ptile, ptile), ptile)
        part = jnp.dot(img[...], wkv[:, columns], preferred_element_type=F32).astype(BF16)
        for n in range(D):
            pb[n, :, columns] = part[n * image_count : (n + 1) * image_count]

    for j in range(1, D):
        n = lax.rem(d + j, D)
        copy = remote(pb.at[n], pb.at[D + d], p_s.at[n], p_r.at[d], {"dp": n})
        copy.start()
        waits.append(copy.wait_send)

    for k in range(2, T - 1):
        for h in range(1, HIDDEN_PARTS):
            hidden_step(k, h)
    for h in range(HIDDEN_PARTS):
        hidden_step(T - 1, h)

    load_query.wait()

    def tokens_of(n):
        if n is None:
            return hb.at[d]
        for h in range(HIDDEN_PARTS):
            remote(
                piece(0, h), piece(T + n, h), hx_s.at[0, h], hx_r.at[n, h], {"dp": n}
            ).wait_recv()
        return hb.at[T + n]

    def project(block, k):
        columns = slice(k * span, (k + 1) * span)
        return jnp.dot(block[...], wq[:, columns], preferred_element_type=F32)

    def query_to_sibling(yy, k):
        return remote(
            qsib.at[yy, k], qsr.at[yy, k], qc_s.at[yy, k], qc_r.at[yy, k], {"dp": sibling}
        )

    def query_to_chip(yy, k, slot):
        return remote(
            qsend.at[yy, k], qr.at[slot, k], qy_s.at[yy, k], qy_r.at[slot, k],
            {"dp": yy * CORES + c},
        )

    order = [0] + list(range(1, Y))
    for j in order:
        yy = lax.rem(y + j, Y)
        block = tokens_of(yy * CORES + 1 - c)
        for k in range(heads_here):
            qsib[yy, k] = project(block, k).astype(BF16)
            query_to_sibling(yy, k).start()
            waits.append(query_to_sibling(yy, k).wait_send)
        if j == 0:
            block = hb.at[d]
            for k in range(heads_here):
                qacc[k] = project(block, k)
            continue
        block = tokens_of(yy * CORES + c)
        for k in range(heads_here):
            part = project(block, k)
            query_to_sibling(yy, k).wait_recv()
            qsend[yy, k] = (part + qsr[yy, k].astype(F32)).astype(BF16)
            query_to_chip(yy, k, y).start()
            waits.append(query_to_chip(yy, k, y).wait_send)

    for j in range(1, D):
        n = lax.rem(d + j, D)
        remote(pb.at[n], pb.at[D + n], p_s.at[n], p_r.at[n], {"dp": n}).wait_recv()
    for j in range(1, T):
        f = lax.rem(t + j, T)
        copy = remote(
            pb.at[jnp.where(f == d, f, D + f)], kvr.at[t], kv_s.at[f], kv_r.at[t], {"tensor": f}
        )
        copy.start()
        waits.append(copy.wait_send)

    load_cot.wait()
    scale = jnp.tanh(jnp.full((1, HEAD_SIZE), gate[0], F32))
    bias_rows = jnp.concatenate([bias[...]] * QUERY_GROUP, axis=0)

    def stack(ref, k):
        first = k * span
        return jnp.concatenate(
            [
                ref[:, first + g * HEAD_SIZE : first + (g + 1) * HEAD_SIZE]
                for g in range(QUERY_GROUP)
            ],
            axis=0,
        )

    for k in range(heads_here):
        above[k] = (scale * stack(cot, k).astype(F32)).astype(BF16)
        query_to_sibling(y, k).wait_recv()
        qacc[k] = qacc[k] + qsr[y, k].astype(F32)
    total = pb[jnp.where(t == d, t, D + t)].astype(F32)
    for j in range(1, T):
        f = lax.rem(t + j, T)
        remote(kvr.at[f], kvr.at[f], kv_s.at[f], kv_r.at[f], {"tensor": f}).wait_recv()
        total = total + kvr[f].astype(F32)
    kvs[...] = total.astype(BF16)
    for k in range(heads_here):
        value = kvs[:, k * pair + HEAD_SIZE : (k + 1) * pair]
        wgrad[k] = lax.dot_general(above[k], value, NT, preferred_element_type=F32)

    scaling = HEAD_SIZE ** (-0.5)

    def grad_piece(f, k):
        return gb.at[f, :, pl.ds(k * pair, pair)]

    def grad_along(f, k, slot, to):
        return remote(
            grad_piece(slot, k), grad_piece(slot, k), g_s.at[f, k], g_r.at[slot, k], {"tensor": to}
        )

    def grad_across(f, k):
        return remote(
            grad_piece(f, k), grad_piece(T + d, k), gx_s.at[f, k], gx_r.at[d, k], {"dp": f}
        )

    for k in range(heads_here):
        key = kvs[:, k * pair : k * pair + HEAD_SIZE]
        query = qacc[k]
        for j in range(1, Y):
            yy = lax.rem(y + j, Y)
            query_to_chip(yy, k, yy).wait_recv()
            query = query + qr[yy, k].astype(F32)
        query = query.astype(BF16)
        stacked = jnp.concatenate(
            [query[:, g * HEAD_SIZE : (g + 1) * HEAD_SIZE] for g in range(QUERY_GROUP)], axis=0
        )
        scores = lax.dot_general(stacked, key, NT, preferred_element_type=F32) * scaling
        scores = scores + bias_rows
        exponent = jnp.exp(scores - jnp.max(scores, axis=-1, keepdims=True))
        weights = exponent / jnp.sum(exponent, axis=-1, keepdims=True)
        low = weights.astype(BF16)
        lows[k] = low
        value_grad = lax.dot_general(low, above[k], TN, preferred_element_type=F32)
        grad_weights = wgrad[k]
        mean = jnp.sum(weights * grad_weights, axis=-1, keepdims=True)
        grad_low = (weights * (grad_weights - mean)).astype(BF16)
        key_grad = lax.dot_general(grad_low, stacked, TN, preferred_element_type=F32) * scaling
        gb[t, :, k * pair : k * pair + HEAD_SIZE] = key_grad.astype(BF16)
        gb[t, :, k * pair + HEAD_SIZE : (k + 1) * pair] = value_grad.astype(BF16)
        for j in range(1, T):
            f = lax.rem(t + j, T)
            grad_along(f, k, t, f).start()
            waits.append(grad_along(f, k, t, f).wait_send)
        pl.when(t != d)(lambda: grad_across(t, k).start())

    for k in range(heads_here):
        value = kvs[:, k * pair + HEAD_SIZE : (k + 1) * pair]
        attended = scale * jnp.dot(lows[k], value, preferred_element_type=F32)
        for g in range(QUERY_GROUP):
            first = k * span + g * HEAD_SIZE
            out[:, first : first + HEAD_SIZE] = attended[g * tokens : (g + 1) * tokens].astype(BF16)

    def grad_arrive(f, k):
        grad_along(f, k, f, f).wait_recv()
        pl.when(f != d)(lambda: grad_across(f, k).start())

    for k in range(heads_here):
        for i in range(1, T):
            pl.when(t - i >= 0)(functools.partial(grad_arrive, t - i, k))
            pl.when(t + i < T)(functools.partial(grad_arrive, t + i, k))

    def grads_of(n):
        if n is None:
            return gb[d]
        for k in range(heads_here):
            remote(
                grad_piece(0, k), grad_piece(T + n, k), gx_s.at[0, k], gx_r.at[n, k], {"dp": n}
            ).wait_recv()
        return gb[T + n]

    def back(block, h):
        weights_part = wkv[h * part_feats : (h + 1) * part_feats, :]
        return lax.dot_general(block, weights_part, NT, preferred_element_type=F32)

    def image_to_sibling(yy, h):
        return remote(
            fsib.at[yy, h], fsr.at[yy, h], fc_s.at[yy, h], fc_r.at[yy, h], {"dp": sibling}
        )

    def image_to_owner(yy, ss, h, slot_y, slot_s):
        return remote(
            fsend.at[yy, ss, h], fr.at[slot_y, slot_s, h],
            f_s.at[yy, ss, h], f_r.at[slot_y, slot_s, h],
            {"section": ss, "dp": yy * CORES + c},
        )

    order = list(range(1, Y)) + [0]
    sections = list(range(1, S)) + [0]
    for j in order:
        yy = lax.rem(y + j, Y)
        block = grads_of(yy * CORES + 1 - c)
        for h in range(GRAD_PARTS):
            fsib[yy, h] = back(block, h).astype(BF16)
            image_to_sibling(yy, h).start()
            waits.append(image_to_sibling(yy, h).wait_send)
    for j in order:
        yy = lax.rem(y + j, Y)
        block = grads_of(None if j == 0 else yy * CORES + c)
        for h in range(GRAD_PARTS):
            part = back(block, h)
            image_to_sibling(yy, h).wait_recv()
            fsum[...] = part + fsr[yy, h].astype(F32)
            for i in sections:
                ss = lax.rem(s + i, S)
                mine = fsum[pl.ds(pl.multiple_of(ss * rows, rows), rows), :]
                if i == 0 and j == 0:
                    grad[:, h * part_feats : (h + 1) * part_feats] = mine
                    continue
                fsend[yy, ss, h] = mine.astype(BF16)
                image_to_owner(yy, ss, h, y, s).start()
                waits.append(image_to_owner(yy, ss, h, y, s).wait_send)
    for h in range(GRAD_PARTS):
        columns = slice(h * part_feats, (h + 1) * part_feats)
        result = grad[:, columns]
        for j in order:
            yy = lax.rem(y + j, Y)
            for i in sections:
                if i == 0 and j == 0:
                    continue
                ss = lax.rem(s + i, S)
                image_to_owner(yy, ss, h, yy, ss).wait_recv()
                result = result + fr[yy, ss, h].astype(F32)
        grad[:, columns] = result

    for wait in waits:
        wait()
    for h in range(HIDDEN_PARTS):
        for k in range(T - 1):
            pl.when((t - k >= 0) & (t + 1 < T))(lambda: right(t - k, h).wait_send())
            pl.when((t + k < T) & (t >= 1))(lambda: left(t + k, h).wait_send())
        for f in range(T):
            pl.when(f != d)(lambda: across(f, h).wait_send())
    for k in range(heads_here):
        for f in range(T):
            pl.when(f != d)(lambda: grad_across(f, k).wait_send())


def local(sizes, hidden, w_query, key_w, value_w, image, bias, gate, cotangent):
    S, D, T = sizes
    Y = D // CORES
    tokens, feats = hidden.shape[1:]
    width = w_query.shape[2]
    kc = key_w.shape[2]
    rows = image.shape[1]
    images = S * rows
    heads = kc // HEAD_SIZE
    span = QUERY_GROUP * HEAD_SIZE
    part_feats = feats // GRAD_PARTS
    sem = lambda *n: pltpu.SemaphoreType.DMA(n)
    any_space = pl.BlockSpec(memory_space=pl.ANY)
    vmem = pl.BlockSpec(memory_space=pltpu.VMEM)
    smem = pl.BlockSpec(memory_space=pltpu.SMEM)
    out, grad = pl.pallas_call(
        functools.partial(kernel, sizes),
        out_shape=(
            jax.ShapeDtypeStruct((tokens, width), BF16),
            jax.ShapeDtypeStruct((rows, feats), F32),
        ),
        in_specs=[any_space] * 5 + [vmem, smem, any_space],
        out_specs=(vmem, vmem),
        scratch_shapes=[
            pltpu.VMEM((feats, width), BF16),
            pltpu.VMEM((feats, 2 * kc), BF16),
            pltpu.VMEM((D * images, feats), BF16),
            pltpu.VMEM((tokens, width), BF16),
            pltpu.VMEM((T + D, tokens, feats), BF16),
            pltpu.VMEM((2 * D, images, 2 * kc), BF16),
            pltpu.VMEM((T, images, 2 * kc), BF16),
            pltpu.VMEM((images, 2 * kc), BF16),
            pltpu.VMEM((Y, heads, tokens, span), BF16),
            pltpu.VMEM((Y, heads, tokens, span), BF16),
            pltpu.VMEM((Y, heads, tokens, span), BF16),
            pltpu.VMEM((Y, heads, tokens, span), BF16),
            pltpu.VMEM((heads, tokens, span), F32),
            pltpu.VMEM((heads, QUERY_GROUP * tokens, HEAD_SIZE), BF16),
            pltpu.VMEM((heads, QUERY_GROUP * tokens, images), F32),
            pltpu.VMEM((heads, QUERY_GROUP * tokens, images), BF16),
            pltpu.VMEM((T + D, images, 2 * kc), BF16),
            pltpu.VMEM((Y, GRAD_PARTS, images, part_feats), BF16),
            pltpu.VMEM((Y, GRAD_PARTS, images, part_feats), BF16),
            pltpu.VMEM((images, part_feats), F32),
            pltpu.VMEM((Y, S, GRAD_PARTS, rows, part_feats), BF16),
            pltpu.VMEM((Y, S, GRAD_PARTS, rows, part_feats), BF16),
            sem(4 + 2 * heads),
            sem(S), sem(S), sem(Y), sem(Y), sem(Y), sem(Y),
            sem(T, HIDDEN_PARTS), sem(T, HIDDEN_PARTS), sem(T, HIDDEN_PARTS),
            sem(T, HIDDEN_PARTS), sem(D, HIDDEN_PARTS),
            sem(D), sem(D), sem(T), sem(T),
            sem(Y, heads), sem(Y, heads), sem(Y, heads), sem(Y, heads),
            sem(T, heads), sem(T, heads), sem(T, heads), sem(D, heads),
            sem(Y, GRAD_PARTS), sem(Y, GRAD_PARTS),
            sem(Y, S, GRAD_PARTS), sem(Y, S, GRAD_PARTS),
        ],
        compiler_params=pltpu.CompilerParams(
            collective_id=0, has_side_effects=True, vmem_limit_bytes=64 * 1024 * 1024 - 64 * 1024
        ),
    )(hidden[0], w_query[0], key_w[0], value_w[0], image[0], bias, gate, cotangent[0])
    return out[None], grad[None]


def solution(mesh):
    sizes = tuple(mesh.shape[name] for name in ("section", "dp", "tensor"))
    assert sizes[1] == sizes[2] and sizes[1] % CORES == 0
    in_specs = (
        P("section", "dp", "tensor"),
        P("section", "dp", "tensor"),
        P("section", "tensor", "dp"),
        P("section", "tensor", "dp"),
        P("dp", "section", "tensor"),
        P("dp", None),
        P("section"),
        P("section", "dp", "tensor"),
    )
    out_specs = (P("section", "dp", "tensor"), P("dp", "section", "tensor"))
    return jax.shard_map(
        functools.partial(local, sizes),
        mesh=mesh, in_specs=in_specs, out_specs=out_specs, check_vma=False,
    )
```

time: 131 us -> 115 us (0.88)
  the two profiles are of different devices: /device:TPU:25 before, /device:TPU:17 now
where the time goes in v2:
time: 115 us; the launch traced here: 114 us
  Pallas kernels  109 us (95%)
  local copies, waits for them, and re-layouts  3.59 us (3%)
  between operations  1.29 us (1%)
    pallas_call x1, Pallas kernels, local(): pl.pallas_call(functools.partial(kernel, sizes), out_shape=(jax.ShapeDtyp...  109 us
    unnamed x2, local copies, waits for them, and re-layouts  3.59 us

profile of v2, /device:TPU:17, one launch (start us, length us, event | category | flops | bytes accessed | tf_op | source)
XLA Modules:
  0.0 113.8 jit_solution(1063462769101881324)
XLA Ops:
  1.3 108.9 %shard_map.95 = (bf16[160,1024]{1,0:T(8,128)(2,1)}, f32[64,2048]{1,0:T(8,128)}) custom-call(bf16[160,2048]{1,0:T(8,128)(2,1)} %bitcast.11, bf16[2048,1024]{1,0:T(8,128)(2,1)} %bitcast.8, bf16[2048,256]{1,0:T(8,128)(2,1)} %bitcast.9, bf16[2048,256]{1,0:T(8,128)(2,1)} %bitcast.10, bf16[64,2048]{1,0:T(8,128)(2,1)} %bitcast.15, f32[160,128]{1,0:T(8,128)} %bias.1, ...), custom_call_target="tpu_custom_call" | custom-call | tf_op jit(solution)/shard_map/pallas_call | solution.py:433
  110.2 1.7 %copy.13 = bf16[1,160,1024]{2,1,0:T(8,128)(2,1)} copy(bf16[1,160,1024]{2,1,0:T(8,128)(2,1)} %bitcast.14) | data formatting | bytes 655360
  111.9 1.9 %copy.14 = f32[1,64,2048]{2,1,0:T(8,128)} copy(f32[1,64,2048]{2,1,0:T(8,128)} %bitcast.12) | data formatting | bytes 1048576

commit v3 on v2

--- a/solution.py
+++ b/solution.py
@@ -9,7 +9,10 @@
 
 HEAD_SIZE = 128
 QUERY_GROUP = 4
-HIDDEN_PARTS = 2
+VMEM_BYTES = 64 * 1024 * 1024 - 64 * 1024
+HALVES = 2
+COLUMN_PARTS = 2
+PIECES = HALVES * COLUMN_PARTS
 GRAD_PARTS = 2
 CORES = 2
 BF16 = jnp.bfloat16
@@ -30,8 +33,8 @@
 
 
 def kernel(
-    sizes, hidden, w_query, key_w, value_w, image, bias, gate, cotangent, out, grad,
-    wq, wkv, img, cot, hb, pb, kvr, kvs, qsib, qsr, qsend, qr, qacc, above, wgrad, lows, gb, fsib, fsr, fsum, fsend, fr,
+    sizes, hidden, w_query, key_w, value_w, image, bias_in, gate, cotangent, out, grad,
+    bias, wq, wkv, img, cot, hb, pb, kvr, kvs, qsib, qsr, qsend, qr, qfull, qacc, lows, gacc, gb, fsib, fsr, ffull, fsum, fsend, fr,
     load, ix_s, ix_r, iy_s, iy_r, ic_s, ic_r, hr_s, hl_s, h_r, hx_s, hx_r, p_s, p_r, kv_s, kv_r,
     qc_s, qc_r, qy_s, qy_r, g_s, g_r, gx_s, gx_r, fc_s, fc_r, f_s, f_r,
 ):
@@ -49,7 +52,8 @@
     pair = 2 * HEAD_SIZE
     span = QUERY_GROUP * HEAD_SIZE
     tokens = bias.shape[0]
-    part_rows = tokens // HIDDEN_PARTS
+    part_rows = tokens // HALVES
+    part_columns = feats // COLUMN_PARTS
     part_feats = feats // GRAD_PARTS
     waits = []
 
@@ -60,7 +64,13 @@
 
     own_rows = pl.ds(pl.multiple_of(d * image_count + s * rows, rows), rows)
     load_image = load_copy(0, image, img.at[own_rows])
-    load_hidden = load_copy(1, hidden, hb.at[t])
+    load_hidden = [
+        load_copy(
+            4 + 2 * heads_here + h, hidden.at[pl.ds(h * part_rows, part_rows)], hb.at[h, t]
+        )
+        for h in range(HALVES)
+    ]
+    load_bias = load_copy(1, bias_in, bias)
     load_query = load_copy(2, w_query, wq)
     load_cot = load_copy(3, cotangent, cot)
     load_pairs = []
@@ -96,10 +106,12 @@
         copy.start()
         waits.append(copy.wait_send)
 
-    load_hidden.wait()
-
-    def piece(f, h):
-        return hb.at[f, pl.ds(h * part_rows, part_rows)]
+    for load_half in load_hidden:
+        load_half.wait()
+
+    def piece(f, p):
+        columns = pl.ds(p % COLUMN_PARTS * part_columns, part_columns)
+        return hb.at[p // COLUMN_PARTS, f, :, columns]
 
     def right(f, h):
         return remote(piece(f, h), piece(f, h), hr_s.at[f, h], h_r.at[f, h], {"tensor": t + 1})
@@ -126,8 +138,15 @@
         hidden_arrive(k, h)
         hidden_pass(k, h)
 
-    for h in range(HIDDEN_PARTS):
-        hidden_pass(0, h)
+    def half(h):
+        return range(h * COLUMN_PARTS, (h + 1) * COLUMN_PARTS)
+
+    def own_across(h):
+        for p in half(h):
+            pl.when(t != d)(lambda: across(t, p).start())
+
+    for p in half(0):
+        hidden_pass(0, p)
 
     def image_block(n):
         return img.at[pl.ds(pl.multiple_of(n * image_count, image_count), image_count)]
@@ -150,10 +169,14 @@
         waits.append(copy.wait_send)
 
     to_sibling(d, y)
-    for h in range(HIDDEN_PARTS):
-        pl.when(t != d)(lambda: across(t, h).start())
-    for h in range(HIDDEN_PARTS):
-        hidden_step(1, h)
+    own_across(0)
+    for k in range(1, T - 1):
+        for p in half(0):
+            hidden_step(k, p)
+    for h in range(1, HALVES):
+        for p in half(h):
+            hidden_pass(0, p)
+        own_across(h)
     for j in range(1, Y):
         src = lax.rem(y + j, Y)
         n = src * CORES + c
@@ -162,8 +185,10 @@
         ).wait_recv()
         to_sibling(n, src)
 
-    for k in range(2, T - 1):
-        hidden_step(k, 0)
+    for p in half(0):
+        hidden_step(T - 1, p)
+    for p in half(1):
+        hidden_step(1, p)
     for j in range(Y):
         n = j * CORES + 1 - c
         remote(
@@ -187,57 +212,61 @@
         waits.append(copy.wait_send)
 
     for k in range(2, T - 1):
-        for h in range(1, HIDDEN_PARTS):
-            hidden_step(k, h)
-    for h in range(HIDDEN_PARTS):
-        hidden_step(T - 1, h)
+        for p in half(1):
+            hidden_step(k, p)
 
     load_query.wait()
 
-    def tokens_of(n):
-        if n is None:
-            return hb.at[d]
-        for h in range(HIDDEN_PARTS):
+    def wait_tokens(n, h):
+        for p in half(h):
             remote(
-                piece(0, h), piece(T + n, h), hx_s.at[0, h], hx_r.at[n, h], {"dp": n}
+                piece(0, p), piece(T + n, p), hx_s.at[0, p], hx_r.at[n, p], {"dp": n}
             ).wait_recv()
-        return hb.at[T + n]
 
     def project(block, k):
         columns = slice(k * span, (k + 1) * span)
-        return jnp.dot(block[...], wq[:, columns], preferred_element_type=F32)
-
-    def query_to_sibling(yy, k):
+        return jnp.dot(block, wq[:, columns], preferred_element_type=F32)
+
+    def query_to_sibling(yy, h, k):
         return remote(
-            qsib.at[yy, k], qsr.at[yy, k], qc_s.at[yy, k], qc_r.at[yy, k], {"dp": sibling}
-        )
-
-    def query_to_chip(yy, k, slot):
+            qsib.at[yy, h, k], qsr.at[yy, h, k], qc_s.at[yy, h, k], qc_r.at[yy, h, k],
+            {"dp": sibling},
+        )
+
+    def query_to_chip(yy, h, k, slot):
         return remote(
-            qsend.at[yy, k], qr.at[slot, k], qy_s.at[yy, k], qy_r.at[slot, k],
+            qsend.at[yy, h, k], qr.at[slot, h, k], qy_s.at[yy, h, k], qy_r.at[slot, h, k],
             {"dp": yy * CORES + c},
         )
 
-    order = [0] + list(range(1, Y))
-    for j in order:
-        yy = lax.rem(y + j, Y)
-        block = tokens_of(yy * CORES + 1 - c)
-        for k in range(heads_here):
-            qsib[yy, k] = project(block, k).astype(BF16)
-            query_to_sibling(yy, k).start()
-            waits.append(query_to_sibling(yy, k).wait_send)
-        if j == 0:
-            block = hb.at[d]
-            for k in range(heads_here):
-                qacc[k] = project(block, k)
-            continue
-        block = tokens_of(yy * CORES + c)
+    def queries(h):
+        wait_tokens(sibling, h)
+        block = jnp.concatenate([hb[h, T + sibling], hb[h, d]], axis=0)
         for k in range(heads_here):
             part = project(block, k)
-            query_to_sibling(yy, k).wait_recv()
-            qsend[yy, k] = (part + qsr[yy, k].astype(F32)).astype(BF16)
-            query_to_chip(yy, k, y).start()
-            waits.append(query_to_chip(yy, k, y).wait_send)
+            qsib[y, h, k] = part[:part_rows].astype(BF16)
+            query_to_sibling(y, h, k).start()
+            waits.append(query_to_sibling(y, h, k).wait_send)
+            qacc[h, k] = part[part_rows:]
+        for j in range(1, Y):
+            yy = lax.rem(y + j, Y)
+            for core in range(CORES):
+                wait_tokens(yy * CORES + core, h)
+            block = hb[h, pl.ds(T + yy * CORES, CORES)].reshape(CORES * part_rows, feats)
+            for k in range(heads_here):
+                qfull[k] = project(block, k).reshape(CORES, part_rows, span)
+                qsib[yy, h, k] = qfull[k, 1 - c].astype(BF16)
+                query_to_sibling(yy, h, k).start()
+                waits.append(query_to_sibling(yy, h, k).wait_send)
+            for k in range(heads_here):
+                query_to_sibling(yy, h, k).wait_recv()
+                qsend[yy, h, k] = (qfull[k, c] + qsr[yy, h, k].astype(F32)).astype(BF16)
+                query_to_chip(yy, h, k, y).start()
+                waits.append(query_to_chip(yy, h, k, y).wait_send)
+
+    queries(0)
+    for p in half(1):
+        hidden_step(T - 1, p)
 
     for j in range(1, D):
         n = lax.rem(d + j, D)
@@ -250,33 +279,15 @@
         copy.start()
         waits.append(copy.wait_send)
 
+    queries(1)
     load_cot.wait()
-    scale = jnp.tanh(jnp.full((1, HEAD_SIZE), gate[0], F32))
-    bias_rows = jnp.concatenate([bias[...]] * QUERY_GROUP, axis=0)
-
-    def stack(ref, k):
-        first = k * span
-        return jnp.concatenate(
-            [
-                ref[:, first + g * HEAD_SIZE : first + (g + 1) * HEAD_SIZE]
-                for g in range(QUERY_GROUP)
-            ],
-            axis=0,
-        )
-
-    for k in range(heads_here):
-        above[k] = (scale * stack(cot, k).astype(F32)).astype(BF16)
-        query_to_sibling(y, k).wait_recv()
-        qacc[k] = qacc[k] + qsr[y, k].astype(F32)
+    load_bias.wait()
     total = pb[jnp.where(t == d, t, D + t)].astype(F32)
     for j in range(1, T):
         f = lax.rem(t + j, T)
         remote(kvr.at[f], kvr.at[f], kv_s.at[f], kv_r.at[f], {"tensor": f}).wait_recv()
         total = total + kvr[f].astype(F32)
     kvs[...] = total.astype(BF16)
-    for k in range(heads_here):
-        value = kvs[:, k * pair + HEAD_SIZE : (k + 1) * pair]
-        wgrad[k] = lax.dot_general(above[k], value, NT, preferred_element_type=F32)
 
     scaling = HEAD_SIZE ** (-0.5)
 
@@ -293,42 +304,70 @@
             grad_piece(f, k), grad_piece(T + d, k), gx_s.at[f, k], gx_r.at[d, k], {"dp": f}
         )
 
-    for k in range(heads_here):
+    scale = jnp.tanh(jnp.full((1, HEAD_SIZE), gate[0], F32))
+
+    def heads_on_rows(block):
+        return jnp.concatenate(
+            [block[:, g * HEAD_SIZE : (g + 1) * HEAD_SIZE] for g in range(QUERY_GROUP)], axis=0
+        )
+
+    def attend(h, k):
+        value = kvs[:, k * pair + HEAD_SIZE : (k + 1) * pair]
+        attended = scale * jnp.dot(lows[k], value, preferred_element_type=F32)
+        for g in range(QUERY_GROUP):
+            first = k * span + g * HEAD_SIZE
+            out[h * part_rows : (h + 1) * part_rows, first : first + HEAD_SIZE] = attended[
+                g * part_rows : (g + 1) * part_rows
+            ].astype(BF16)
+
+    def attention(h, k):
+        half_rows = slice(h * part_rows, (h + 1) * part_rows)
         key = kvs[:, k * pair : k * pair + HEAD_SIZE]
-        query = qacc[k]
+        value = kvs[:, k * pair + HEAD_SIZE : (k + 1) * pair]
+        above = heads_on_rows(cot[half_rows, k * span : (k + 1) * span])
+        above = (scale * above.astype(F32)).astype(BF16)
+        grad_weights = lax.dot_general(above, value, NT, preferred_element_type=F32)
+        bias_rows = jnp.concatenate([bias[half_rows, :]] * QUERY_GROUP, axis=0)
+        query_to_sibling(y, h, k).wait_recv()
+        query = qacc[h, k] + qsr[y, h, k].astype(F32)
         for j in range(1, Y):
             yy = lax.rem(y + j, Y)
-            query_to_chip(yy, k, yy).wait_recv()
-            query = query + qr[yy, k].astype(F32)
-        query = query.astype(BF16)
-        stacked = jnp.concatenate(
-            [query[:, g * HEAD_SIZE : (g + 1) * HEAD_SIZE] for g in range(QUERY_GROUP)], axis=0
-        )
+            query_to_chip(yy, h, k, yy).wait_recv()
+            query = query + qr[yy, h, k].astype(F32)
+        stacked = heads_on_rows(query.astype(BF16))
         scores = lax.dot_general(stacked, key, NT, preferred_element_type=F32) * scaling
         scores = scores + bias_rows
         exponent = jnp.exp(scores - jnp.max(scores, axis=-1, keepdims=True))
         weights = exponent / jnp.sum(exponent, axis=-1, keepdims=True)
         low = weights.astype(BF16)
         lows[k] = low
-        value_grad = lax.dot_general(low, above[k], TN, preferred_element_type=F32)
-        grad_weights = wgrad[k]
+        value_grad = lax.dot_general(low, above, TN, preferred_element_type=F32)
         mean = jnp.sum(weights * grad_weights, axis=-1, keepdims=True)
         grad_low = (weights * (grad_weights - mean)).astype(BF16)
-        key_grad = lax.dot_general(grad_low, stacked, TN, preferred_element_type=F32) * scaling
-        gb[t, :, k * pair : k * pair + HEAD_SIZE] = key_grad.astype(BF16)
-        gb[t, :, k * pair + HEAD_SIZE : (k + 1) * pair] = value_grad.astype(BF16)
-        for j in range(1, T):
-            f = lax.rem(t + j, T)
-            grad_along(f, k, t, f).start()
-            waits.append(grad_along(f, k, t, f).wait_send)
-        pl.when(t != d)(lambda: grad_across(t, k).start())
-
+        key_grad = lax.dot_general(grad_low, stacked, TN, preferred_element_type=F32)
+        return key_grad, value_grad
+
+    for h in range(HALVES):
+        last = h == HALVES - 1
+        for k in range(heads_here):
+            key_grad, value_grad = attention(h, k)
+            if h:
+                key_grad = key_grad + gacc[k, 0]
+                value_grad = value_grad + gacc[k, 1]
+            if not last:
+                gacc[k, 0] = key_grad
+                gacc[k, 1] = value_grad
+                attend(h, k)
+                continue
+            gb[t, :, k * pair : k * pair + HEAD_SIZE] = (key_grad * scaling).astype(BF16)
+            gb[t, :, k * pair + HEAD_SIZE : (k + 1) * pair] = value_grad.astype(BF16)
+            for j in range(1, T):
+                f = lax.rem(t + j, T)
+                grad_along(f, k, t, f).start()
+                waits.append(grad_along(f, k, t, f).wait_send)
+            pl.when(t != d)(lambda: grad_across(t, k).start())
     for k in range(heads_here):
-        value = kvs[:, k * pair + HEAD_SIZE : (k + 1) * pair]
-        attended = scale * jnp.dot(lows[k], value, preferred_element_type=F32)
-        for g in range(QUERY_GROUP):
-            first = k * span + g * HEAD_SIZE
-            out[:, first : first + HEAD_SIZE] = attended[g * tokens : (g + 1) * tokens].astype(BF16)
+        attend(HALVES - 1, k)
 
     def grad_arrive(f, k):
         grad_along(f, k, f, f).wait_recv()
@@ -339,14 +378,11 @@
             pl.when(t - i >= 0)(functools.partial(grad_arrive, t - i, k))
             pl.when(t + i < T)(functools.partial(grad_arrive, t + i, k))
 
-    def grads_of(n):
-        if n is None:
-            return gb[d]
+    def wait_grads(n):
         for k in range(heads_here):
             remote(
                 grad_piece(0, k), grad_piece(T + n, k), gx_s.at[0, k], gx_r.at[n, k], {"dp": n}
             ).wait_recv()
-        return gb[T + n]
 
     def back(block, h):
         weights_part = wkv[h * part_feats : (h + 1) * part_feats, :]
@@ -368,18 +404,23 @@
     sections = list(range(1, S)) + [0]
     for j in order:
         yy = lax.rem(y + j, Y)
-        block = grads_of(yy * CORES + 1 - c)
+        if j:
+            for core in range(CORES):
+                wait_grads(yy * CORES + core)
+            block = gb[pl.ds(T + yy * CORES, CORES)].reshape(CORES * image_count, 2 * kc)
+            given, kept = 1 - c, c
+        else:
+            wait_grads(sibling)
+            block = jnp.concatenate([gb[T + sibling], gb[d]], axis=0)
+            given, kept = 0, 1
         for h in range(GRAD_PARTS):
-            fsib[yy, h] = back(block, h).astype(BF16)
+            ffull[h] = back(block, h).reshape(CORES, image_count, part_feats)
+            fsib[yy, h] = ffull[h, given].astype(BF16)
             image_to_sibling(yy, h).start()
             waits.append(image_to_sibling(yy, h).wait_send)
-    for j in order:
-        yy = lax.rem(y + j, Y)
-        block = grads_of(None if j == 0 else yy * CORES + c)
         for h in range(GRAD_PARTS):
-            part = back(block, h)
             image_to_sibling(yy, h).wait_recv()
-            fsum[...] = part + fsr[yy, h].astype(F32)
+            fsum[...] = ffull[h, kept] + fsr[yy, h].astype(F32)
             for i in sections:
                 ss = lax.rem(s + i, S)
                 mine = fsum[pl.ds(pl.multiple_of(ss * rows, rows), rows), :]
@@ -404,7 +445,7 @@
 
     for wait in waits:
         wait()
-    for h in range(HIDDEN_PARTS):
+    for h in range(PIECES):
         for k in range(T - 1):
             pl.when((t - k >= 0) & (t + 1 < T))(lambda: right(t - k, h).wait_send())
             pl.when((t + k < T) & (t >= 1))(lambda: left(t + k, h).wait_send())
@@ -413,6 +454,17 @@
     for k in range(heads_here):
         for f in range(T):
             pl.when(f != d)(lambda: grad_across(f, k).wait_send())
+
+
+def finish(out, grad, out_result, grad_result, sems):
+    copies = [
+        pltpu.make_async_copy(out, out_result, sems.at[0]),
+        pltpu.make_async_copy(grad, grad_result, sems.at[1]),
+    ]
+    for copy in copies:
+        copy.start()
+    for copy in copies:
+        copy.wait()
 
 
 def local(sizes, hidden, w_query, key_w, value_w, image, bias, gate, cotangent):
@@ -425,9 +477,10 @@
     images = S * rows
     heads = kc // HEAD_SIZE
     span = QUERY_GROUP * HEAD_SIZE
+    part_rows = tokens // HALVES
     part_feats = feats // GRAD_PARTS
     sem = lambda *n: pltpu.SemaphoreType.DMA(n)
-    any_space = pl.BlockSpec(memory_space=pl.ANY)
+    hbm = pl.BlockSpec(memory_space=pl.ANY)
     vmem = pl.BlockSpec(memory_space=pltpu.VMEM)
     smem = pl.BlockSpec(memory_space=pltpu.SMEM)
     out, grad = pl.pallas_call(
@@ -436,45 +489,58 @@
             jax.ShapeDtypeStruct((tokens, width), BF16),
             jax.ShapeDtypeStruct((rows, feats), F32),
         ),
-        in_specs=[any_space] * 5 + [vmem, smem, any_space],
+        in_specs=[hbm] * 6 + [smem, hbm],
         out_specs=(vmem, vmem),
         scratch_shapes=[
+            pltpu.VMEM((tokens, images), F32),
             pltpu.VMEM((feats, width), BF16),
             pltpu.VMEM((feats, 2 * kc), BF16),
             pltpu.VMEM((D * images, feats), BF16),
             pltpu.VMEM((tokens, width), BF16),
-            pltpu.VMEM((T + D, tokens, feats), BF16),
+            pltpu.VMEM((HALVES, T + D, part_rows, feats), BF16),
             pltpu.VMEM((2 * D, images, 2 * kc), BF16),
             pltpu.VMEM((T, images, 2 * kc), BF16),
             pltpu.VMEM((images, 2 * kc), BF16),
-            pltpu.VMEM((Y, heads, tokens, span), BF16),
-            pltpu.VMEM((Y, heads, tokens, span), BF16),
-            pltpu.VMEM((Y, heads, tokens, span), BF16),
-            pltpu.VMEM((Y, heads, tokens, span), BF16),
-            pltpu.VMEM((heads, tokens, span), F32),
-            pltpu.VMEM((heads, QUERY_GROUP * tokens, HEAD_SIZE), BF16),
-            pltpu.VMEM((heads, QUERY_GROUP * tokens, images), F32),
-            pltpu.VMEM((heads, QUERY_GROUP * tokens, images), BF16),
+            pltpu.VMEM((Y, HALVES, heads, part_rows, span), BF16),
+            pltpu.VMEM((Y, HALVES, heads, part_rows, span), BF16),
+            pltpu.VMEM((Y, HALVES, heads, part_rows, span), BF16),
+            pltpu.VMEM((Y, HALVES, heads, part_rows, span), BF16),
+            pltpu.VMEM((heads, CORES, part_rows, span), F32),
+            pltpu.VMEM((HALVES, heads, part_rows, span), F32),
+            pltpu.VMEM((heads, QUERY_GROUP * part_rows, images), BF16),
+            pltpu.VMEM((heads, 2, images, HEAD_SIZE), F32),
             pltpu.VMEM((T + D, images, 2 * kc), BF16),
             pltpu.VMEM((Y, GRAD_PARTS, images, part_feats), BF16),
             pltpu.VMEM((Y, GRAD_PARTS, images, part_feats), BF16),
+            pltpu.VMEM((GRAD_PARTS, CORES, images, part_feats), F32),
             pltpu.VMEM((images, part_feats), F32),
             pltpu.VMEM((Y, S, GRAD_PARTS, rows, part_feats), BF16),
             pltpu.VMEM((Y, S, GRAD_PARTS, rows, part_feats), BF16),
-            sem(4 + 2 * heads),
+            sem(4 + 2 * heads + HALVES),
             sem(S), sem(S), sem(Y), sem(Y), sem(Y), sem(Y),
-            sem(T, HIDDEN_PARTS), sem(T, HIDDEN_PARTS), sem(T, HIDDEN_PARTS),
-            sem(T, HIDDEN_PARTS), sem(D, HIDDEN_PARTS),
+            sem(T, PIECES), sem(T, PIECES), sem(T, PIECES), sem(T, PIECES), sem(D, PIECES),
             sem(D), sem(D), sem(T), sem(T),
-            sem(Y, heads), sem(Y, heads), sem(Y, heads), sem(Y, heads),
+            sem(Y, HALVES, heads), sem(Y, HALVES, heads),
+            sem(Y, HALVES, heads), sem(Y, HALVES, heads),
             sem(T, heads), sem(T, heads), sem(T, heads), sem(D, heads),
             sem(Y, GRAD_PARTS), sem(Y, GRAD_PARTS),
             sem(Y, S, GRAD_PARTS), sem(Y, S, GRAD_PARTS),
         ],
         compiler_params=pltpu.CompilerParams(
-            collective_id=0, has_side_effects=True, vmem_limit_bytes=64 * 1024 * 1024 - 64 * 1024
+            collective_id=0, has_side_effects=True, vmem_limit_bytes=VMEM_BYTES
         ),
     )(hidden[0], w_query[0], key_w[0], value_w[0], image[0], bias, gate, cotangent[0])
+    out, grad = pl.pallas_call(
+        finish,
+        out_shape=(
+            jax.ShapeDtypeStruct((tokens, width), BF16),
+            jax.ShapeDtypeStruct((rows, feats), F32),
+        ),
+        in_specs=[hbm, hbm],
+        out_specs=(hbm, hbm),
+        scratch_shapes=[sem(2)],
+        compiler_params=pltpu.CompilerParams(vmem_limit_bytes=VMEM_BYTES),
+    )(out, grad)
     return out[None], grad[None]
 
 

time: 115 us -> 135 us (1.17); the launches traced: 114 us -> 132 us
  Pallas kernels: 109 us -> 131 us
  local copies, waits for them, and re-layouts: 3.59 us -> 0 us
    pallas_call x0 -> x1, Pallas kernels: none -> 26.9 us  [local(): pl.pallas_call(finish, out_shape=(jax.ShapeDtypeStruct((tokens, width), B...]
    pallas_call x1, Pallas kernels: 109 us -> 104 us  [local(): pl.pallas_call(functools.partial(kernel, sizes), out_shape=(jax.ShapeDtyp...]
    unnamed x2 -> x0, local copies, waits for them, and re-layouts: 3.59 us -> none
where the time goes in v3:
time: 135 us; the launch traced here: 132 us
  Pallas kernels  131 us (97%)
    pallas_call x1, Pallas kernels, local(): pl.pallas_call(functools.partial(kernel, sizes), out_shape=(jax.ShapeDtyp...  104 us
    pallas_call x1, Pallas kernels, local(): pl.pallas_call(finish, out_shape=(jax.ShapeDtypeStruct((tokens, width), B...  26.9 us

profile of v3, /device:TPU:17, one launch (start us, length us, event | category | flops | bytes accessed | tf_op | source)
XLA Modules:
  0.0 132.3 jit_solution(3395941083603707713)
XLA Ops:
  1.3 104.1 %shard_map.95 = (bf16[160,1024]{1,0:T(8,128)(2,1)}, f32[64,2048]{1,0:T(8,128)}) custom-call(bf16[160,2048]{1,0:T(8,128)(2,1)} %bitcast.11, bf16[2048,1024]{1,0:T(8,128)(2,1)} %bitcast.8, bf16[2048,256]{1,0:T(8,128)(2,1)} %bitcast.9, bf16[2048,256]{1,0:T(8,128)(2,1)} %bitcast.10, bf16[64,2048]{1,0:T(8,128)(2,1)} %bitcast.13, f32[160,128]{1,0:T(8,128)} %bias_in.1, ...), custom_call_target="tpu_custom_call" | custom-call | tf_op jit(solution)/shard_map/pallas_call | solution.py:486
  105.4 26.9 %shard_map.96 = (bf16[160,1024]{1,0:T(8,128)(2,1)}, f32[64,2048]{1,0:T(8,128)}) custom-call(bf16[160,1024]{1,0:T(8,128)(2,1)} %get-tuple-element.6.out, f32[64,2048]{1,0:T(8,128)} %get-tuple-element.7.grad), custom_call_target="tpu_custom_call" | custom-call | tf_op jit(solution)/shard_map/pallas_call | solution.py:533

commit v4 on v3

--- a/solution.py
+++ b/solution.py
@@ -34,7 +34,7 @@
 
 def kernel(
     sizes, hidden, w_query, key_w, value_w, image, bias_in, gate, cotangent, out, grad,
-    bias, wq, wkv, img, cot, hb, pb, kvr, kvs, qsib, qsr, qsend, qr, qfull, qacc, lows, gacc, gb, fsib, fsr, ffull, fsum, fsend, fr,
+    bias, wq, wkv, wkvt, img, cot, hb, pb, kvr, kvs, qsib, qsr, qsend, qr, qfull, qacc, above, wgrad, lows, gacc, gb, fsib, fsr, ffull, fsum, fsend, fr,
     load, ix_s, ix_r, iy_s, iy_r, ic_s, ic_r, hr_s, hl_s, h_r, hx_s, hx_r, p_s, p_r, kv_s, kv_r,
     qc_s, qc_r, qy_s, qy_r, g_s, g_r, gx_s, gx_r, fc_s, fc_r, f_s, f_r,
 ):
@@ -177,6 +177,10 @@
         for p in half(h):
             hidden_pass(0, p)
         own_across(h)
+    for load_pair in load_pairs:
+        load_pair.wait()
+    for i in range(0, feats, 2 * kc):
+        wkvt[:, i : i + 2 * kc] = wkv[i : i + 2 * kc, :].T
     for j in range(1, Y):
         src = lax.rem(y + j, Y)
         n = src * CORES + c
@@ -194,8 +198,6 @@
         remote(
             image_block(n), image_block(n), ic_s.at[j], ic_r.at[j], {"dp": sibling}
         ).wait_recv()
-    for load_pair in load_pairs:
-        load_pair.wait()
     ptile = min(256, 2 * kc)
 
     @pl.loop(0, 2 * kc // ptile)
@@ -264,30 +266,47 @@
                 query_to_chip(yy, h, k, y).start()
                 waits.append(query_to_chip(yy, h, k, y).wait_send)
 
-    queries(0)
-    for p in half(1):
-        hidden_step(T - 1, p)
-
     for j in range(1, D):
         n = lax.rem(d + j, D)
         remote(pb.at[n], pb.at[D + n], p_s.at[n], p_r.at[n], {"dp": n}).wait_recv()
-    for j in range(1, T):
-        f = lax.rem(t + j, T)
-        copy = remote(
+
+    def pairs_to(f):
+        return remote(
             pb.at[jnp.where(f == d, f, D + f)], kvr.at[t], kv_s.at[f], kv_r.at[t], {"tensor": f}
         )
-        copy.start()
-        waits.append(copy.wait_send)
-
-    queries(1)
+
+    for f in range(1, T - 1):
+        pl.when(t != f)(lambda: pairs_to(f).start())
     load_cot.wait()
     load_bias.wait()
+    scale = jnp.tanh(jnp.full((1, HEAD_SIZE), gate[0], F32))
+    queries(0)
+    for f in (0, T - 1):
+        pl.when(t != f)(lambda: pairs_to(f).start())
+
+    def heads_on_rows(block):
+        return jnp.concatenate(
+            [block[:, g * HEAD_SIZE : (g + 1) * HEAD_SIZE] for g in range(QUERY_GROUP)], axis=0
+        )
+
+    for h in range(HALVES):
+        for k in range(heads_here):
+            rows_here = cot[h * part_rows : (h + 1) * part_rows, k * span : (k + 1) * span]
+            above[h, k] = (scale * heads_on_rows(rows_here).astype(F32)).astype(BF16)
+    for p in half(1):
+        hidden_step(T - 1, p)
+
+    queries(1)
     total = pb[jnp.where(t == d, t, D + t)].astype(F32)
     for j in range(1, T):
         f = lax.rem(t + j, T)
         remote(kvr.at[f], kvr.at[f], kv_s.at[f], kv_r.at[f], {"tensor": f}).wait_recv()
         total = total + kvr[f].astype(F32)
     kvs[...] = total.astype(BF16)
+    for h in range(HALVES):
+        for k in range(heads_here):
+            value = kvs[:, k * pair + HEAD_SIZE : (k + 1) * pair]
+            wgrad[h, k] = lax.dot_general(above[h, k], value, NT, preferred_element_type=F32)
 
     scaling = HEAD_SIZE ** (-0.5)
 
@@ -302,13 +321,6 @@
     def grad_across(f, k):
         return remote(
             grad_piece(f, k), grad_piece(T + d, k), gx_s.at[f, k], gx_r.at[d, k], {"dp": f}
-        )
-
-    scale = jnp.tanh(jnp.full((1, HEAD_SIZE), gate[0], F32))
-
-    def heads_on_rows(block):
-        return jnp.concatenate(
-            [block[:, g * HEAD_SIZE : (g + 1) * HEAD_SIZE] for g in range(QUERY_GROUP)], axis=0
         )
 
     def attend(h, k):
@@ -323,10 +335,7 @@
     def attention(h, k):
         half_rows = slice(h * part_rows, (h + 1) * part_rows)
         key = kvs[:, k * pair : k * pair + HEAD_SIZE]
-        value = kvs[:, k * pair + HEAD_SIZE : (k + 1) * pair]
-        above = heads_on_rows(cot[half_rows, k * span : (k + 1) * span])
-        above = (scale * above.astype(F32)).astype(BF16)
-        grad_weights = lax.dot_general(above, value, NT, preferred_element_type=F32)
+        grad_weights = wgrad[h, k]
         bias_rows = jnp.concatenate([bias[half_rows, :]] * QUERY_GROUP, axis=0)
         query_to_sibling(y, h, k).wait_recv()
         query = qacc[h, k] + qsr[y, h, k].astype(F32)
@@ -338,10 +347,10 @@
         scores = lax.dot_general(stacked, key, NT, preferred_element_type=F32) * scaling
         scores = scores + bias_rows
         exponent = jnp.exp(scores - jnp.max(scores, axis=-1, keepdims=True))
-        weights = exponent / jnp.sum(exponent, axis=-1, keepdims=True)
+        weights = exponent * (1.0 / jnp.sum(exponent, axis=-1, keepdims=True))
         low = weights.astype(BF16)
         lows[k] = low
-        value_grad = lax.dot_general(low, above, TN, preferred_element_type=F32)
+        value_grad = lax.dot_general(low, above[h, k], TN, preferred_element_type=F32)
         mean = jnp.sum(weights * grad_weights, axis=-1, keepdims=True)
         grad_low = (weights * (grad_weights - mean)).astype(BF16)
         key_grad = lax.dot_general(grad_low, stacked, TN, preferred_element_type=F32)
@@ -385,8 +394,8 @@
             ).wait_recv()
 
     def back(block, h):
-        weights_part = wkv[h * part_feats : (h + 1) * part_feats, :]
-        return lax.dot_general(block, weights_part, NT, preferred_element_type=F32)
+        weights_part = wkvt[:, h * part_feats : (h + 1) * part_feats]
+        return jnp.dot(block, weights_part, preferred_element_type=F32)
 
     def image_to_sibling(yy, h):
         return remote(
@@ -451,19 +460,25 @@
             pl.when((t + k < T) & (t >= 1))(lambda: left(t + k, h).wait_send())
         for f in range(T):
             pl.when(f != d)(lambda: across(f, h).wait_send())
+    for f in range(T):
+        pl.when(t != f)(lambda: pairs_to(f).wait_send())
     for k in range(heads_here):
         for f in range(T):
             pl.when(f != d)(lambda: grad_across(f, k).wait_send())
 
 
-def finish(out, grad, out_result, grad_result, sems):
-    copies = [
-        pltpu.make_async_copy(out, out_result, sems.at[0]),
-        pltpu.make_async_copy(grad, grad_result, sems.at[1]),
-    ]
-    for copy in copies:
+def finish(out, grad, out_result, grad_result, out_held, grad_held, sems):
+    arrays = [(out, out_held, out_result), (grad, grad_held, grad_result)]
+    inward, outward = [], []
+    for i, (source, held, result) in enumerate(arrays):
+        inward.append(pltpu.make_async_copy(source, held, sems.at[i, 0]))
+        outward.append(pltpu.make_async_copy(held, result, sems.at[i, 1]))
+    for copy in inward:
         copy.start()
-    for copy in copies:
+    for first, second in zip(inward, outward):
+        first.wait()
+        second.start()
+    for copy in outward:
         copy.wait()
 
 
@@ -495,6 +510,7 @@
             pltpu.VMEM((tokens, images), F32),
             pltpu.VMEM((feats, width), BF16),
             pltpu.VMEM((feats, 2 * kc), BF16),
+            pltpu.VMEM((2 * kc, feats), BF16),
             pltpu.VMEM((D * images, feats), BF16),
             pltpu.VMEM((tokens, width), BF16),
             pltpu.VMEM((HALVES, T + D, part_rows, feats), BF16),
@@ -507,6 +523,8 @@
             pltpu.VMEM((Y, HALVES, heads, part_rows, span), BF16),
             pltpu.VMEM((heads, CORES, part_rows, span), F32),
             pltpu.VMEM((HALVES, heads, part_rows, span), F32),
+            pltpu.VMEM((HALVES, heads, QUERY_GROUP * part_rows, HEAD_SIZE), BF16),
+            pltpu.VMEM((HALVES, heads, QUERY_GROUP * part_rows, images), F32),
             pltpu.VMEM((heads, QUERY_GROUP * part_rows, images), BF16),
             pltpu.VMEM((heads, 2, images, HEAD_SIZE), F32),
             pltpu.VMEM((T + D, images, 2 * kc), BF16),
@@ -538,7 +556,11 @@
         ),
         in_specs=[hbm, hbm],
         out_specs=(hbm, hbm),
-        scratch_shapes=[sem(2)],
+        scratch_shapes=[
+            pltpu.VMEM((tokens, width), BF16),
+            pltpu.VMEM((rows, feats), F32),
+            sem(2, 2),
+        ],
         compiler_params=pltpu.CompilerParams(vmem_limit_bytes=VMEM_BYTES),
     )(out, grad)
     return out[None], grad[None]

time: 135 us -> 114 us (0.84); the launches traced: 132 us -> 114 us
  Pallas kernels: 131 us -> 113 us
    pallas_call x1, Pallas kernels: 26.9 us -> 1.97 us  [local(): pl.pallas_call(finish, out_shape=(jax.ShapeDtypeStruct((tokens, width), B...]
    pallas_call x1, Pallas kernels: 104 us -> 111 us  [local(): pl.pallas_call(functools.partial(kernel, sizes), out_shape=(jax.ShapeDtyp...]
where the time goes in v4:
time: 114 us
  Pallas kernels  113 us (99%)
  between operations  1.29 us (1%)
    pallas_call x1, Pallas kernels, local(): pl.pallas_call(functools.partial(kernel, sizes), out_shape=(jax.ShapeDtyp...  111 us

profile of v4, /device:TPU:17, one launch (start us, length us, event | category | flops | bytes accessed | tf_op | source)
XLA Modules:
  0.0 114.1 jit_solution(827331310911272370)
XLA Ops:
  1.3 110.9 %shard_map.95 = (bf16[160,1024]{1,0:T(8,128)(2,1)}, f32[64,2048]{1,0:T(8,128)}) custom-call(bf16[160,2048]{1,0:T(8,128)(2,1)} %bitcast.11, bf16[2048,1024]{1,0:T(8,128)(2,1)} %bitcast.8, bf16[2048,256]{1,0:T(8,128)(2,1)} %bitcast.9, bf16[2048,256]{1,0:T(8,128)(2,1)} %bitcast.10, bf16[64,2048]{1,0:T(8,128)(2,1)} %bitcast.13, f32[160,128]{1,0:T(8,128)} %bias_in.1, ...), custom_call_target="tpu_custom_call" | custom-call | tf_op jit(solution)/shard_map/pallas_call | solution.py:501
  112.2 2.0 %shard_map.96 = (bf16[160,1024]{1,0:T(8,128)(2,1)}, f32[64,2048]{1,0:T(8,128)}) custom-call(bf16[160,1024]{1,0:T(8,128)(2,1)} %get-tuple-element.6.out, f32[64,2048]{1,0:T(8,128)} %get-tuple-element.7.grad), custom_call_target="tpu_custom_call" | custom-call | tf_op jit(solution)/shard_map/pallas_call | solution.py:551

commit v5 on v4

--- a/solution.py
+++ b/solution.py
@@ -34,7 +34,7 @@
 
 def kernel(
     sizes, hidden, w_query, key_w, value_w, image, bias_in, gate, cotangent, out, grad,
-    bias, wq, wkv, wkvt, img, cot, hb, pb, kvr, kvs, qsib, qsr, qsend, qr, qfull, qacc, above, wgrad, lows, gacc, gb, fsib, fsr, ffull, fsum, fsend, fr,
+    bias, wq, wkv, img, cot, hb, pb, kvr, kvs, qsib, qsr, qsend, qr, qfull, qacc, above, wgrad, lows, gacc, gb, fsib, fsr, ffull, fsum, fsend, fr,
     load, ix_s, ix_r, iy_s, iy_r, ic_s, ic_r, hr_s, hl_s, h_r, hx_s, hx_r, p_s, p_r, kv_s, kv_r,
     qc_s, qc_r, qy_s, qy_r, g_s, g_r, gx_s, gx_r, fc_s, fc_r, f_s, f_r,
 ):
@@ -173,14 +173,16 @@
     for k in range(1, T - 1):
         for p in half(0):
             hidden_step(k, p)
-    for h in range(1, HALVES):
-        for p in half(h):
-            hidden_pass(0, p)
-        own_across(h)
-    for load_pair in load_pairs:
-        load_pair.wait()
-    for i in range(0, feats, 2 * kc):
-        wkvt[:, i : i + 2 * kc] = wkv[i : i + 2 * kc, :].T
+    for p in half(1):
+        hidden_pass(0, p)
+    for p in half(1):
+        hidden_step(1, p)
+    for p in half(0):
+        hidden_step(T - 1, p)
+    own_across(1)
+    for k in range(2, T - 1):
+        for p in half(1):
+            hidden_step(k, p)
     for j in range(1, Y):
         src = lax.rem(y + j, Y)
         n = src * CORES + c
@@ -189,15 +191,13 @@
         ).wait_recv()
         to_sibling(n, src)
 
-    for p in half(0):
-        hidden_step(T - 1, p)
-    for p in half(1):
-        hidden_step(1, p)
     for j in range(Y):
         n = j * CORES + 1 - c
         remote(
             image_block(n), image_block(n), ic_s.at[j], ic_r.at[j], {"dp": sibling}
         ).wait_recv()
+    for load_pair in load_pairs:
+        load_pair.wait()
     ptile = min(256, 2 * kc)
 
     @pl.loop(0, 2 * kc // ptile)
@@ -213,9 +213,6 @@
         copy.start()
         waits.append(copy.wait_send)
 
-    for k in range(2, T - 1):
-        for p in half(1):
-            hidden_step(k, p)
 
     load_query.wait()
 
@@ -266,6 +263,8 @@
                 query_to_chip(yy, h, k, y).start()
                 waits.append(query_to_chip(yy, h, k, y).wait_send)
 
+    queries(0)
+
     for j in range(1, D):
         n = lax.rem(d + j, D)
         remote(pb.at[n], pb.at[D + n], p_s.at[n], p_r.at[n], {"dp": n}).wait_recv()
@@ -277,12 +276,14 @@
 
     for f in range(1, T - 1):
         pl.when(t != f)(lambda: pairs_to(f).start())
+    for p in half(1):
+        hidden_step(T - 1, p)
+    for f in (0, T - 1):
+        pl.when(t != f)(lambda: pairs_to(f).start())
+    queries(1)
     load_cot.wait()
     load_bias.wait()
     scale = jnp.tanh(jnp.full((1, HEAD_SIZE), gate[0], F32))
-    queries(0)
-    for f in (0, T - 1):
-        pl.when(t != f)(lambda: pairs_to(f).start())
 
     def heads_on_rows(block):
         return jnp.concatenate(
@@ -293,10 +294,7 @@
         for k in range(heads_here):
             rows_here = cot[h * part_rows : (h + 1) * part_rows, k * span : (k + 1) * span]
             above[h, k] = (scale * heads_on_rows(rows_here).astype(F32)).astype(BF16)
-    for p in half(1):
-        hidden_step(T - 1, p)
-
-    queries(1)
+
     total = pb[jnp.where(t == d, t, D + t)].astype(F32)
     for j in range(1, T):
         f = lax.rem(t + j, T)
@@ -394,8 +392,8 @@
             ).wait_recv()
 
     def back(block, h):
-        weights_part = wkvt[:, h * part_feats : (h + 1) * part_feats]
-        return jnp.dot(block, weights_part, preferred_element_type=F32)
+        weights_part = wkv[h * part_feats : (h + 1) * part_feats, :]
+        return lax.dot_general(block, weights_part, NT, preferred_element_type=F32)
 
     def image_to_sibling(yy, h):
         return remote(
@@ -510,7 +508,6 @@
             pltpu.VMEM((tokens, images), F32),
             pltpu.VMEM((feats, width), BF16),
             pltpu.VMEM((feats, 2 * kc), BF16),
-            pltpu.VMEM((2 * kc, feats), BF16),
             pltpu.VMEM((D * images, feats), BF16),
             pltpu.VMEM((tokens, width), BF16),
             pltpu.VMEM((HALVES, T + D, part_rows, feats), BF16),

time: 114 us -> 107 us (0.939)
  Pallas kernels: 113 us -> 106 us
    pallas_call x1, Pallas kernels: 111 us -> 104 us  [local(): pl.pallas_call(functools.partial(kernel, sizes), out_shape=(jax.ShapeDtyp...]
where the time goes in v5:
time: 107 us
  Pallas kernels  106 us (99%)
  between operations  1.29 us (1%)
    pallas_call x1, Pallas kernels, local(): pl.pallas_call(functools.partial(kernel, sizes), out_shape=(jax.ShapeDtyp...  104 us

profile of v5, /device:TPU:17, one launch (start us, length us, event | category | flops | bytes accessed | tf_op | source)
XLA Modules:
  0.0 107.2 jit_solution(1015507994014167546)
XLA Ops:
  1.3 103.9 %shard_map.95 = (bf16[160,1024]{1,0:T(8,128)(2,1)}, f32[64,2048]{1,0:T(8,128)}) custom-call(bf16[160,2048]{1,0:T(8,128)(2,1)} %bitcast.11, bf16[2048,1024]{1,0:T(8,128)(2,1)} %bitcast.8, bf16[2048,256]{1,0:T(8,128)(2,1)} %bitcast.9, bf16[2048,256]{1,0:T(8,128)(2,1)} %bitcast.10, bf16[64,2048]{1,0:T(8,128)(2,1)} %bitcast.13, f32[160,128]{1,0:T(8,128)} %bias_in.1, ...), custom_call_target="tpu_custom_call" | custom-call | tf_op jit(solution)/shard_map/pallas_call | solution.py:499
  105.2 2.0 %shard_map.96 = (bf16[160,1024]{1,0:T(8,128)(2,1)}, f32[64,2048]{1,0:T(8,128)}) custom-call(bf16[160,1024]{1,0:T(8,128)(2,1)} %get-tuple-element.6.out, f32[64,2048]{1,0:T(8,128)} %get-tuple-element.7.grad), custom_call_target="tpu_custom_call" | custom-call | tf_op jit(solution)/shard_map/pallas_call | solution.py:548

commit v6 on v5

--- a/solution.py
+++ b/solution.py
@@ -19,6 +19,11 @@
 F32 = jnp.float32
 NT = (((1,), (1,)), ((), ()))
 TN = (((0,), (0,)), ((), ()))
+
+
+def row_parts(tokens):
+    first = tokens * 3 // 5 // 16 * 16
+    return (0, first), (first, tokens - first)
 
 
 def remote(src, dst, send_sem, recv_sem, device):
@@ -52,7 +57,7 @@
     pair = 2 * HEAD_SIZE
     span = QUERY_GROUP * HEAD_SIZE
     tokens = bias.shape[0]
-    part_rows = tokens // HALVES
+    parts = row_parts(tokens)
     part_columns = feats // COLUMN_PARTS
     part_feats = feats // GRAD_PARTS
     waits = []
@@ -66,7 +71,7 @@
     load_image = load_copy(0, image, img.at[own_rows])
     load_hidden = [
         load_copy(
-            4 + 2 * heads_here + h, hidden.at[pl.ds(h * part_rows, part_rows)], hb.at[h, t]
+            4 + 2 * heads_here + h, hidden.at[pl.ds(*parts[h])], hb.at[h, t, pl.ds(0, parts[h][1])]
         )
         for h in range(HALVES)
     ]
@@ -111,7 +116,8 @@
 
     def piece(f, p):
         columns = pl.ds(p % COLUMN_PARTS * part_columns, part_columns)
-        return hb.at[p // COLUMN_PARTS, f, :, columns]
+        h = p // COLUMN_PARTS
+        return hb.at[h, f, pl.ds(0, parts[h][1]), columns]
 
     def right(f, h):
         return remote(piece(f, h), piece(f, h), hr_s.at[f, h], h_r.at[f, h], {"tensor": t + 1})
@@ -227,39 +233,44 @@
         return jnp.dot(block, wq[:, columns], preferred_element_type=F32)
 
     def query_to_sibling(yy, h, k):
+        held = pl.ds(0, parts[h][1])
         return remote(
-            qsib.at[yy, h, k], qsr.at[yy, h, k], qc_s.at[yy, h, k], qc_r.at[yy, h, k],
+            qsib.at[yy, h, k, held], qsr.at[yy, h, k, held], qc_s.at[yy, h, k], qc_r.at[yy, h, k],
             {"dp": sibling},
         )
 
     def query_to_chip(yy, h, k, slot):
+        held = pl.ds(0, parts[h][1])
         return remote(
-            qsend.at[yy, h, k], qr.at[slot, h, k], qy_s.at[yy, h, k], qy_r.at[slot, h, k],
+            qsend.at[yy, h, k, held], qr.at[slot, h, k, held], qy_s.at[yy, h, k], qy_r.at[slot, h, k],
             {"dp": yy * CORES + c},
         )
 
     def queries(h):
+        count = parts[h][1]
         wait_tokens(sibling, h)
-        block = jnp.concatenate([hb[h, T + sibling], hb[h, d]], axis=0)
+        block = jnp.concatenate([hb[h, T + sibling, :count], hb[h, d, :count]], axis=0)
         for k in range(heads_here):
             part = project(block, k)
-            qsib[y, h, k] = part[:part_rows].astype(BF16)
+            qsib[y, h, k, :count] = part[:count].astype(BF16)
             query_to_sibling(y, h, k).start()
             waits.append(query_to_sibling(y, h, k).wait_send)
-            qacc[h, k] = part[part_rows:]
+            qacc[h, k, :count] = part[count:]
         for j in range(1, Y):
             yy = lax.rem(y + j, Y)
             for core in range(CORES):
                 wait_tokens(yy * CORES + core, h)
-            block = hb[h, pl.ds(T + yy * CORES, CORES)].reshape(CORES * part_rows, feats)
+            block = hb[h, pl.ds(T + yy * CORES, CORES), :count]
+            block = block.reshape(CORES * count, feats)
             for k in range(heads_here):
-                qfull[k] = project(block, k).reshape(CORES, part_rows, span)
-                qsib[yy, h, k] = qfull[k, 1 - c].astype(BF16)
+                qfull[k, :, :count] = project(block, k).reshape(CORES, count, span)
+                qsib[yy, h, k, :count] = qfull[k, 1 - c, :count].astype(BF16)
                 query_to_sibling(yy, h, k).start()
                 waits.append(query_to_sibling(yy, h, k).wait_send)
             for k in range(heads_here):
                 query_to_sibling(yy, h, k).wait_recv()
-                qsend[yy, h, k] = (qfull[k, c] + qsr[yy, h, k].astype(F32)).astype(BF16)
+                total = qfull[k, c, :count] + qsr[yy, h, k, :count].astype(F32)
+                qsend[yy, h, k, :count] = total.astype(BF16)
                 query_to_chip(yy, h, k, y).start()
                 waits.append(query_to_chip(yy, h, k, y).wait_send)
 
@@ -276,25 +287,26 @@
 
     for f in range(1, T - 1):
         pl.when(t != f)(lambda: pairs_to(f).start())
+    load_cot.wait()
+    load_bias.wait()
+    scale = jnp.tanh(jnp.full((1, HEAD_SIZE), gate[0], F32))
+
+    def heads_on_rows(block):
+        return jnp.concatenate(
+            [block[:, g * HEAD_SIZE : (g + 1) * HEAD_SIZE] for g in range(QUERY_GROUP)], axis=0
+        )
+
+    for h in range(HALVES):
+        for k in range(heads_here):
+            first, count = parts[h]
+            rows_here = cot[first : first + count, k * span : (k + 1) * span]
+            above[h, k, : QUERY_GROUP * count] = (scale * heads_on_rows(rows_here).astype(F32)).astype(BF16)
+
     for p in half(1):
         hidden_step(T - 1, p)
     for f in (0, T - 1):
         pl.when(t != f)(lambda: pairs_to(f).start())
     queries(1)
-    load_cot.wait()
-    load_bias.wait()
-    scale = jnp.tanh(jnp.full((1, HEAD_SIZE), gate[0], F32))
-
-    def heads_on_rows(block):
-        return jnp.concatenate(
-            [block[:, g * HEAD_SIZE : (g + 1) * HEAD_SIZE] for g in range(QUERY_GROUP)], axis=0
-        )
-
-    for h in range(HALVES):
-        for k in range(heads_here):
-            rows_here = cot[h * part_rows : (h + 1) * part_rows, k * span : (k + 1) * span]
-            above[h, k] = (scale * heads_on_rows(rows_here).astype(F32)).astype(BF16)
-
     total = pb[jnp.where(t == d, t, D + t)].astype(F32)
     for j in range(1, T):
         f = lax.rem(t + j, T)
@@ -304,7 +316,10 @@
     for h in range(HALVES):
         for k in range(heads_here):
             value = kvs[:, k * pair + HEAD_SIZE : (k + 1) * pair]
-            wgrad[h, k] = lax.dot_general(above[h, k], value, NT, preferred_element_type=F32)
+            stacked_rows = QUERY_GROUP * parts[h][1]
+            wgrad[h, k, :stacked_rows] = lax.dot_general(
+                above[h, k, :stacked_rows], value, NT, preferred_element_type=F32
+            )
 
     scaling = HEAD_SIZE ** (-0.5)
 
@@ -323,37 +338,42 @@
 
     def attend(h, k):
         value = kvs[:, k * pair + HEAD_SIZE : (k + 1) * pair]
-        attended = scale * jnp.dot(lows[k], value, preferred_element_type=F32)
+        first_row, count = parts[h]
+        attended = scale * jnp.dot(
+            lows[k, : QUERY_GROUP * count], value, preferred_element_type=F32
+        )
         for g in range(QUERY_GROUP):
             first = k * span + g * HEAD_SIZE
-            out[h * part_rows : (h + 1) * part_rows, first : first + HEAD_SIZE] = attended[
-                g * part_rows : (g + 1) * part_rows
+            out[first_row : first_row + count, first : first + HEAD_SIZE] = attended[
+                g * count : (g + 1) * count
             ].astype(BF16)
 
     def attention(h, k):
-        half_rows = slice(h * part_rows, (h + 1) * part_rows)
+        first_row, count = parts[h]
+        stacked_rows = QUERY_GROUP * count
         key = kvs[:, k * pair : k * pair + HEAD_SIZE]
-        grad_weights = wgrad[h, k]
-        bias_rows = jnp.concatenate([bias[half_rows, :]] * QUERY_GROUP, axis=0)
+        grad_weights = wgrad[h, k, :stacked_rows]
+        bias_rows = jnp.concatenate([bias[first_row : first_row + count, :]] * QUERY_GROUP, axis=0)
         query_to_sibling(y, h, k).wait_recv()
-        query = qacc[h, k] + qsr[y, h, k].astype(F32)
+        query = qacc[h, k, :count] + qsr[y, h, k, :count].astype(F32)
         for j in range(1, Y):
             yy = lax.rem(y + j, Y)
             query_to_chip(yy, h, k, yy).wait_recv()
-            query = query + qr[yy, h, k].astype(F32)
+            query = query + qr[yy, h, k, :count].astype(F32)
         stacked = heads_on_rows(query.astype(BF16))
         scores = lax.dot_general(stacked, key, NT, preferred_element_type=F32) * scaling
         scores = scores + bias_rows
         exponent = jnp.exp(scores - jnp.max(scores, axis=-1, keepdims=True))
         weights = exponent * (1.0 / jnp.sum(exponent, axis=-1, keepdims=True))
         low = weights.astype(BF16)
-        lows[k] = low
-        value_grad = lax.dot_general(low, above[h, k], TN, preferred_element_type=F32)
+        lows[k, :stacked_rows] = low
+        value_grad = lax.dot_general(low, above[h, k, :stacked_rows], TN, preferred_element_type=F32)
         mean = jnp.sum(weights * grad_weights, axis=-1, keepdims=True)
         grad_low = (weights * (grad_weights - mean)).astype(BF16)
         key_grad = lax.dot_general(grad_low, stacked, TN, preferred_element_type=F32)
         return key_grad, value_grad
 
+    grad_waits = []
     for h in range(HALVES):
         last = h == HALVES - 1
         for k in range(heads_here):
@@ -371,10 +391,22 @@
             for j in range(1, T):
                 f = lax.rem(t + j, T)
                 grad_along(f, k, t, f).start()
-                waits.append(grad_along(f, k, t, f).wait_send)
+                grad_waits.append(grad_along(f, k, t, f).wait_send)
             pl.when(t != d)(lambda: grad_across(t, k).start())
     for k in range(heads_here):
         attend(HALVES - 1, k)
+
+    for wait in waits:
+        wait()
+    for h in range(PIECES):
+        for k in range(T - 1):
+            pl.when((t - k >= 0) & (t + 1 < T))(lambda: right(t - k, h).wait_send())
+            pl.when((t + k < T) & (t >= 1))(lambda: left(t + k, h).wait_send())
+        for f in range(T):
+            pl.when(f != d)(lambda: across(f, h).wait_send())
+    for f in range(T):
+        pl.when(t != f)(lambda: pairs_to(f).wait_send())
+    waits = list(grad_waits)
 
     def grad_arrive(f, k):
         grad_along(f, k, f, f).wait_recv()
@@ -452,14 +484,6 @@
 
     for wait in waits:
         wait()
-    for h in range(PIECES):
-        for k in range(T - 1):
-            pl.when((t - k >= 0) & (t + 1 < T))(lambda: right(t - k, h).wait_send())
-            pl.when((t + k < T) & (t >= 1))(lambda: left(t + k, h).wait_send())
-        for f in range(T):
-            pl.when(f != d)(lambda: across(f, h).wait_send())
-    for f in range(T):
-        pl.when(t != f)(lambda: pairs_to(f).wait_send())
     for k in range(heads_here):
         for f in range(T):
             pl.when(f != d)(lambda: grad_across(f, k).wait_send())
@@ -490,7 +514,7 @@
     images = S * rows
     heads = kc // HEAD_SIZE
     span = QUERY_GROUP * HEAD_SIZE
-    part_rows = tokens // HALVES
+    part_rows = max(count for _, count in row_parts(tokens))
     part_feats = feats // GRAD_PARTS
     sem = lambda *n: pltpu.SemaphoreType.DMA(n)
     hbm = pl.BlockSpec(memory_space=pl.ANY)

time: 107 us -> 106 us (level)
  no operation moved by 1% of the time
where the time goes in v6:
time: 106 us
  Pallas kernels  105 us (99%)
  between operations  1.29 us (1%)
    pallas_call x1, Pallas kernels, local(): pl.pallas_call(functools.partial(kernel, sizes), out_shape=(jax.ShapeDtyp...  103 us

profile of v6, /device:TPU:17, one launch (start us, length us, event | category | flops | bytes accessed | tf_op | source)
XLA Modules:
  0.0 106.1 jit_solution(12287942189724081306)
XLA Ops:
  1.3 102.9 %shard_map.95 = (bf16[160,1024]{1,0:T(8,128)(2,1)}, f32[64,2048]{1,0:T(8,128)}) custom-call(bf16[160,2048]{1,0:T(8,128)(2,1)} %bitcast.11, bf16[2048,1024]{1,0:T(8,128)(2,1)} %bitcast.8, bf16[2048,256]{1,0:T(8,128)(2,1)} %bitcast.9, bf16[2048,256]{1,0:T(8,128)(2,1)} %bitcast.10, bf16[64,2048]{1,0:T(8,128)(2,1)} %bitcast.13, f32[160,128]{1,0:T(8,128)} %bias_in.1, ...), custom_call_target="tpu_custom_call" | custom-call | tf_op jit(solution)/shard_map/pallas_call | solution.py:523
  104.1 2.0 %shard_map.96 = (bf16[160,1024]{1,0:T(8,128)(2,1)}, f32[64,2048]{1,0:T(8,128)}) custom-call(bf16[160,1024]{1,0:T(8,128)(2,1)} %get-tuple-element.6.out, f32[64,2048]{1,0:T(8,128)} %get-tuple-element.7.grad), custom_call_target="tpu_custom_call" | custom-call | tf_op jit(solution)/shard_map/pallas_call | solution.py:572

commit v7 on v6

--- a/solution.py
+++ b/solution.py
@@ -287,6 +287,8 @@
 
     for f in range(1, T - 1):
         pl.when(t != f)(lambda: pairs_to(f).start())
+    for f in (0, T - 1):
+        pl.when(t != f)(lambda: pairs_to(f).start())
     load_cot.wait()
     load_bias.wait()
     scale = jnp.tanh(jnp.full((1, HEAD_SIZE), gate[0], F32))
@@ -304,8 +306,6 @@
 
     for p in half(1):
         hidden_step(T - 1, p)
-    for f in (0, T - 1):
-        pl.when(t != f)(lambda: pairs_to(f).start())
     queries(1)
     total = pb[jnp.where(t == d, t, D + t)].astype(F32)
     for j in range(1, T):

time: 106 us -> 106 us (level)
  no operation moved by 1% of the time
where the time goes in v7:
time: 106 us
  Pallas kernels  105 us (99%)
  between operations  1.29 us (1%)
    pallas_call x1, Pallas kernels, local(): pl.pallas_call(functools.partial(kernel, sizes), out_shape=(jax.ShapeDtyp...  103 us

profile of v7, /device:TPU:17, one launch (start us, length us, event | category | flops | bytes accessed | tf_op | source)
XLA Modules:
  0.0 106.1 jit_solution(10666671567687726085)
XLA Ops:
  1.3 102.9 %shard_map.95 = (bf16[160,1024]{1,0:T(8,128)(2,1)}, f32[64,2048]{1,0:T(8,128)}) custom-call(bf16[160,2048]{1,0:T(8,128)(2,1)} %bitcast.11, bf16[2048,1024]{1,0:T(8,128)(2,1)} %bitcast.8, bf16[2048,256]{1,0:T(8,128)(2,1)} %bitcast.9, bf16[2048,256]{1,0:T(8,128)(2,1)} %bitcast.10, bf16[64,2048]{1,0:T(8,128)(2,1)} %bitcast.13, f32[160,128]{1,0:T(8,128)} %bias_in.1, ...), custom_call_target="tpu_custom_call" | custom-call | tf_op jit(solution)/shard_map/pallas_call | solution.py:523
  104.1 2.0 %shard_map.96 = (bf16[160,1024]{1,0:T(8,128)(2,1)}, f32[64,2048]{1,0:T(8,128)}) custom-call(bf16[160,1024]{1,0:T(8,128)(2,1)} %get-tuple-element.6.out, f32[64,2048]{1,0:T(8,128)} %get-tuple-element.7.grad), custom_call_target="tpu_custom_call" | custom-call | tf_op jit(solution)/shard_map/pallas_call | solution.py:572
